TPU v7x, 1024 devices: a whole 4x8x16 slice. The times are simulated.
1024 devices in a mesh: gx: 32 (over z, core), gy: 32 (over x, y).
Axes of the slice: x: 4, y: 8, z: 16, core: 2. Of those that a mesh axis runs over, the one named last changes fastest.
Arguments:
- vorticity: float32 [38, 4096, 4096], P(None, 'gx', 'gy'), may hold values from 0.05 to 20
Outputs:
- leaders_fine: float32 [36, 2048, 2048], P(None, 'gx', 'gy')
- leaders_middle: float32 [36, 1024, 1024], P(None, 'gx', 'gy')
- leaders_coarse: float32 [36, 512, 512], P(None, 'gx', 'gy')
All inputs are finite; a program needn't handle non-finite values.
Results may differ from a plain program's by a relative error of at most 0.000082.
Values sent between devices are 32-bit elements; how exact they have to be, the bound alone decides.
A program may use at most 64 MiB of HBM per device.

v0:
```python
import jax
import jax.numpy as jnp
from jax import lax
from jax.sharding import PartitionSpec as P

LEVELS = 3


LOW_TAPS = (
    0.3326705529509569,
    0.8068915093133388,
    0.4598775021193313,
    -0.13501102001039084,
    -0.08544127388224149,
    0.035226291882100656,
)
HIGH_TAPS = (
    0.035226291882100656,
    0.08544127388224149,
    -0.13501102001039084,
    -0.4598775021193313,
    0.8068915093133388,
    -0.3326705529509569,
)


def passed_along(x, axis, by):
    devices = lax.axis_size(axis)
    return lax.ppermute(x, axis, [(i, (i + by) % devices) for i in range(devices)])


def with_halo(cells, sides, width):
    for axis, dim in sides:
        count = lax.axis_size(axis)
        head = lax.slice_in_dim(cells, 0, width, axis=dim)
        tail = lax.slice_in_dim(cells, cells.shape[dim] - width, cells.shape[dim], axis=dim)
        cells = jnp.concatenate(
            [
                lax.ppermute(tail, axis, [(i, (i + 1) % count) for i in range(count)]),
                cells,
                lax.ppermute(head, axis, [((i + 1) % count, i) for i in range(count)]),
            ],
            axis=dim,
        )
    return cells


def band_matrix(length, number):
    row_ids = lax.broadcasted_iota(jnp.int32, (length, number), 0)
    col_ids = lax.broadcasted_iota(jnp.int32, (length, number), 1)
    offset = row_ids - 2 * col_ids
    low_part = jnp.zeros((length, number), jnp.float32)
    high_part = jnp.zeros((length, number), jnp.float32)
    for tap_index in range(len(LOW_TAPS)):
        low_part = low_part + jnp.where(offset == tap_index, LOW_TAPS[tap_index], 0.0).astype(
            jnp.float32
        )
        high_part = high_part + jnp.where(offset == tap_index, HIGH_TAPS[tap_index], 0.0).astype(
            jnp.float32
        )
    return jnp.concatenate([low_part, high_part], axis=1)


def split_x(values, number):
    matrix = band_matrix(values.shape[1], number)
    return jnp.einsum("zxy,xk->zky", values, matrix, precision=lax.Precision.HIGHEST)


def split_y(values, number):
    planes, length_x, length_y = values.shape
    matrix = band_matrix(length_y, number)
    combined = jnp.dot(
        values.reshape(planes * length_x, length_y), matrix, precision=lax.Precision.HIGHEST
    )
    return combined.reshape(planes, length_x, 2 * number)


def quadrants(combined, number_x, number_y):
    smooth = combined[:, :number_x, :number_y]
    detail = jnp.maximum(
        jnp.abs(combined[:, :number_x, number_y:]), jnp.abs(combined[:, number_x:, :number_y])
    )
    detail = jnp.maximum(detail, jnp.abs(combined[:, number_x:, number_y:]))
    return (smooth, detail)


def depth_max(values):
    return jnp.maximum(jnp.maximum(values[:-2], values[1:-1]), values[2:])


def pool_pairs(values):
    planes, size_x, size_y = values.shape
    half_x = size_x // 2
    half_y = size_y // 2
    return jnp.max(values.reshape(planes, half_x, 2, half_y, 2), axis=(2, 4))


def box_max(framed):
    along_x = jnp.maximum(jnp.maximum(framed[:, :-2, :], framed[:, 1:-1, :]), framed[:, 2:, :])
    return jnp.maximum(jnp.maximum(along_x[:, :, :-2], along_x[:, :, 1:-1]), along_x[:, :, 2:])


def leaders_from(magnitudes, frame_fn):
    outputs = []
    carried = None
    for level_index in range(len(magnitudes)):
        stacked = depth_max(magnitudes[level_index])
        if level_index > 0:
            pooled = pool_pairs(carried)
            stacked = jnp.maximum(stacked, pooled)
        carried = stacked
        outputs.append(box_max(frame_fn(stacked, level_index)))
    return (outputs[0], outputs[1], outputs[2])


def shards(vorticity):
    border_width = len(LOW_TAPS) - 2
    smooth = vorticity
    magnitudes = []
    for level_index in range(LEVELS):
        half_x = smooth.shape[1] // 2
        half_y = smooth.shape[2] // 2
        border = passed_along(smooth[:, :border_width, :], "gx", -1)
        combined = split_x(jnp.concatenate([smooth, border], axis=1), half_x)
        border = passed_along(combined[:, :, :border_width], "gy", -1)
        combined = split_y(jnp.concatenate([combined, border], axis=2), half_y)
        smooth, detail = quadrants(combined, half_x, half_y)
        magnitudes.append(detail)

    def frame_level(stacked, level_index):
        return with_halo(stacked, (("gx", 1), ("gy", 2)), 1)

    return leaders_from(magnitudes, frame_level)


def solution(mesh):
    placed = (P(None, "gx", "gy"),)
    return jax.shard_map(
        shards,
        mesh=mesh,
        in_specs=placed,
        out_specs=(P(None, "gx", "gy"), P(None, "gx", "gy"), P(None, "gx", "gy")),
        check_vma=False,
    )
```

profile of v0, /device:TPU:62, one launch (start us, length us, event | category | flops | bytes accessed | tf_op | source)
XLA Modules:
  0.0 142.4 jit_solution(10727675343946553823)
XLA Ops:
  1.6 15.8 %collective-permute-start = (f32[38,4,128]{2,1,0:T(4,128)S(1)}, f32[38,4,128]{2,1,0:T(4,128)S(1)}, u32[]{:S(2)}, u32[]{:S(2)}) collective-permute-start(f32[38,4,128]{2,1,0:T(4,128)S(1)} %slice.170), channel_id=1, source_target_pairs={{0,992},{32,0},{64,32},{96,64},{128,96},{160,128},{192,160},{224,1... | collective-permute-start | bytes 233480 | tf_op jit(solution)/shard_map/ppermute | solution.py:29
  19.3 9.9 %fusion.8 = f32[38,128,128]{1,2,0:T(8,128)S(1)} fusion(f32[38,4,128]{2,1,0:T(4,128)S(1)} %collective-permute-done, f32[38,128,128]{2,1,0:T(8,128)} %param.1, f32[132,64]{1,0:T(8,128)S(1)} %get-tuple-element.33, f32[132,64]{1,0:T(8,128)S(1)} %get-tuple-element.32), kind=kOutput, calls=%fused_computation.8 | convolution fusion | flops 986844672 | bytes 5126144 | tf_op jit(solution)/shard_map/zxy,xk->zky/dot_general | solution.py:66
  29.3 3.4 %collective-permute-start.1 = (f32[38,128,4]{1,2,0:T(4,128)S(1)}, f32[38,128,4]{1,2,0:T(4,128)S(1)}, u32[]{:S(2)}, u32[]{:S(2)}) collective-permute-start(f32[38,128,4]{1,2,0:T(4,128)S(1)} %slice.226), channel_id=1, source_target_pairs={{0,31},{1,0},{2,1},{3,2},{4,3},{5,4},{6,5},{7,6},{8,7},{9,8},{10,9... | collective-permute-start | bytes 233480 | tf_op jit(solution)/shard_map/ppermute | solution.py:29
  32.8 6.1 %collective-permute-done.1 = f32[38,128,4]{1,2,0:T(4,128)S(1)} collective-permute-done((f32[38,128,4]{1,2,0:T(4,128)S(1)}, f32[38,128,4]{1,2,0:T(4,128)S(1)}, u32[]{:S(2)}, u32[]{:S(2)}) %collective-permute-start.1) | collective-permute-done | bytes 77856 | tf_op jit(solution)/shard_map/ppermute | solution.py:29
  38.9 8.1 %fusion.4 = f32[38,128,128]{2,1,0:T(8,128)S(1)} fusion(f32[38,128,4]{1,2,0:T(4,128)S(1)} %collective-permute-done.1, f32[38,128,128]{1,2,0:T(8,128)S(1)} %fusion.8, f32[132,64]{1,0:T(8,128)S(1)} %get-tuple-element.33, f32[132,64]{1,0:T(8,128)S(1)} %get-tuple-element.32), kind=kOutput, calls=%fused_computation.4 | convolution fusion | flops 986844672 | bytes 5126144 | tf_op jit(solution)/shard_map/dot_general | solution.py:72
  48.9 2.9 %collective-permute-start.3 = (f32[36,1,64]{2,1,0:T(1,128)S(1)}, f32[36,1,64]{2,1,0:T(1,128)S(1)}, u32[]{:S(2)}, u32[]{:S(2)}) collective-permute-start(f32[36,1,64]{2,1,0:T(1,128)S(1)} %get-tuple-element.19), channel_id=1, source_target_pairs={{32,0},{64,32},{96,64},{128,96},{160,128},{192,160},{224,192},{256... | collective-permute-start | bytes 27656 | tf_op jit(solution)/shard_map/ppermute | solution.py:41
  56.8 1.9 %collective-permute-start.4 = (f32[36,66,1]{1,2,0:T(1,128)S(1)}, f32[36,66,1]{1,2,0:T(1,128)}, u32[]{:S(2)}, u32[]{:S(2)}) collective-permute-start(f32[36,66,1]{1,2,0:T(1,128)S(1)} %copy.14), channel_id=1, source_target_pairs={{0,1},{1,2},{2,3},{3,4},{4,5},{5,6},{6,7},{7,8},{8,9},{9,10},{10,1... | collective-permute-start | bytes 28520 | tf_op jit(solution)/shard_map/ppermute | solution.py:39
  59.9 4.1 %collective-permute-start.5 = (f32[36,66,1]{1,2,0:T(1,128)}, f32[36,66,1]{1,2,0:T(1,128)}, u32[]{:S(2)}, u32[]{:S(2)}) collective-permute-start(f32[36,66,1]{1,2,0:T(1,128)} %copy.15), channel_id=1, source_target_pairs={{1,0},{2,1},{3,2},{4,3},{5,4},{6,5},{7,6},{8,7},{9,8},{10,9},{11,1... | collective-permute-start | bytes 28520 | tf_op jit(solution)/shard_map/ppermute | solution.py:41
  65.6 2.8 %reduce_max.18 = f32[36,32,32]{0,2,1:T(8,128)} reduce(f32[36,32,2,32,2]{0,4,3,2,1:T(2,128)S(1)} %bitcast.24, f32[]{:T(128)} %constant.4.clone.1), dimensions={2,4}, to_apply=%region_0.1 | reduce | flops 110592 | bytes 737284 | tf_op jit(solution)/shard_map/reduce_max | solution.py:95
  68.4 2.4 %copy.22 = f32[36,32,32]{2,1,0:T(8,128)} copy(f32[36,32,32]{0,2,1:T(8,128)} %reduce_max.18) | data formatting | bytes 294912 | tf_op jit(solution)/shard_map/reduce_max | solution.py:95
  70.7 2.3 %copy.16 = f32[36,66,1]{2,1,0:T(8,128)} copy(f32[36,66,1]{1,2,0:T(1,128)} %collective-permute-done.4) | data formatting | bytes 19008 | tf_op jit(solution)/shard_map/ppermute | solution.py:39
  73.1 2.3 %copy.17 = f32[36,66,1]{2,1,0:T(8,128)} copy(f32[36,66,1]{1,2,0:T(1,128)} %collective-permute-done.5) | data formatting | bytes 19008 | tf_op jit(solution)/shard_map/ppermute | solution.py:41
  75.4 2.4 %convolution_bitcast_fusion = f32[38,64,64]{2,1,0:T(8,128)S(1)} fusion(f32[38,4,64]{2,1,0:T(4,128)S(1)} %collective-permute-done.6, f32[38,64,64]{2,1,0:T(8,128)} %get-tuple-element.12, f32[68,32]{0,1:T(8,128)S(1)} %get-tuple-element.31, f32[68,32]{0,1:T(8,128)S(1)} %get-tuple-element.30), kind=kOutput, calls=%fused_computation.9 | convolution fusion | flops 127178496 | bytes 1301504 | tf_op jit(solution)/shard_map/zxy,xk->zky/dot_general | solution.py:66
  80.8 2.6 %pad_maximum_fusion.1 = f32[36,66,66]{2,1,0:T(8,128)S(1)} fusion(f32[36,66,1]{2,1,0:T(8,128)} %copy.17, f32[36,1,64]{2,1,0:T(1,128)S(1)} %collective-permute-done.3, f32[36,64,64]{2,1,0:T(8,128)S(1)} %slice_maximum_fusion.4, f32[36,1,64]{2,1,0:T(1,128)S(1)} %collective-permute-done.2, f32[36,66,1]{2,1,0:T(8,128)} %copy.16), kind=kLoop, calls=%fused_computation.14 | loop fusion | flops 627264 | bytes 1254528 | tf_op jit(solution)/shard_map/concatenate | solution.py:37
  83.3 5.1 %collective-permute-done.7 = f32[38,64,4]{1,2,0:T(4,128)S(1)} collective-permute-done((f32[38,64,4]{1,2,0:T(4,128)S(1)}, f32[38,64,4]{1,2,0:T(4,128)S(1)}, u32[]{:S(2)}, u32[]{:S(2)}) %collective-permute-start.7) | collective-permute-done | bytes 38944 | tf_op jit(solution)/shard_map/ppermute | solution.py:29
  88.9 2.5 %fusion.16 = f32[38,64,64]{2,1,0:T(8,128)S(1)} fusion(f32[38,64,4]{2,1,0:T(8,128)S(1)} %copy.20, f32[38,64,64]{2,1,0:T(8,128)} %copy-done, f32[68,32]{0,1:T(8,128)S(1)} %get-tuple-element.31, f32[68,32]{0,1:T(8,128)S(1)} %get-tuple-element.30), kind=kOutput, calls=%fused_computation.20 | convolution fusion | flops 127178496 | bytes 1301504 | tf_op jit(solution)/shard_map/dot_general | solution.py:72
  92.8 2.9 %collective-permute-start.9 = (f32[36,1,32]{2,1,0:T(1,128)S(1)}, f32[36,1,32]{2,1,0:T(1,128)S(1)}, u32[]{:S(2)}, u32[]{:S(2)}) collective-permute-start(f32[36,1,32]{2,1,0:T(1,128)S(1)} %get-tuple-element.23), channel_id=1, source_target_pairs={{32,0},{64,32},{96,64},{128,96},{160,128},{192,160},{224,192},{256... | collective-permute-start | bytes 13832 | tf_op jit(solution)/shard_map/ppermute | solution.py:41
  99.7 2.1 %collective-permute-start.10 = (f32[36,34,1]{0,2,1:T(1,128)}, f32[36,34,1]{0,2,1:T(1,128)S(1)}, u32[]{:S(2)}, u32[]{:S(2)}) collective-permute-start(f32[36,34,1]{0,2,1:T(1,128)} %copy.23), channel_id=1, source_target_pairs={{0,1},{1,2},{2,3},{3,4},{4,5},{5,6},{6,7},{7,8},{8,9},{9,10},{10,1... | collective-permute-start | bytes 14696 | tf_op jit(solution)/shard_map/ppermute | solution.py:39
  102.2 4.0 %collective-permute-start.11 = (f32[36,34,1]{0,2,1:T(1,128)S(1)}, f32[36,34,1]{0,2,1:T(1,128)}, u32[]{:S(2)}, u32[]{:S(2)}) collective-permute-start(f32[36,34,1]{0,2,1:T(1,128)S(1)} %copy.24), channel_id=1, source_target_pairs={{1,0},{2,1},{3,2},{4,3},{5,4},{6,5},{7,6},{8,7},{9,8},{10,9},{11,1... | collective-permute-start | bytes 14696 | tf_op jit(solution)/shard_map/ppermute | solution.py:41
  113.2 2.6 %convolution_bitcast_fusion.1 = f32[38,32,32]{0,1,2:T(8,128)S(1)} fusion(f32[38,36,32]{1,0,2:T(8,128)S(1)} %copy.27, f32[36,16]{0,1:T(8,128)S(1)} %copy-done.4, f32[36,16]{0,1:T(8,128)S(1)} %get-tuple-element.28), kind=kOutput, calls=%fused_computation.24 | convolution fusion | flops 16811136 | bytes 335360 | tf_op jit(solution)/shard_map/zxy,xk->zky/dot_general | solution.py:66
  118.3 7.0 %collective-permute-done.13 = f32[38,32,4]{0,1,2:T(8,128)S(1)} collective-permute-done((f32[38,32,4]{0,1,2:T(8,128)S(1)}, f32[38,32,4]{0,1,2:T(8,128)S(1)}, u32[]{:S(2)}, u32[]{:S(2)}) %collective-permute-start.13) | collective-permute-done | bytes 19488 | tf_op jit(solution)/shard_map/ppermute | solution.py:29
  126.5 2.9 %collective-permute-start.15 = (f32[36,1,16]{0,2,1:T(8,128)S(1)}, f32[36,1,16]{0,2,1:T(8,128)S(1)}, u32[]{:S(2)}, u32[]{:S(2)}) collective-permute-start(f32[36,1,16]{0,2,1:T(8,128)S(1)} %get-tuple-element.27), channel_id=1, source_target_pairs={{32,0},{64,32},{96,64},{128,96},{160,128},{192,160},{224,192},{256... | collective-permute-start | bytes 6920 | tf_op jit(solution)/shard_map/ppermute | solution.py:41
  132.8 3.9 %collective-permute-start.17 = (f32[36,18,1]{0,2,1:T(1,128)S(1)}, f32[36,18,1]{0,2,1:T(1,128)S(1)}, u32[]{:S(2)}, u32[]{:S(2)}) collective-permute-start(f32[36,18,1]{0,2,1:T(1,128)S(1)} %get-tuple-element.25), channel_id=1, source_target_pairs={{1,0},{2,1},{3,2},{4,3},{5,4},{6,5},{7,6},{8,7},{9,8},{10,9},{11,1... | collective-permute-start | bytes 7784 | tf_op jit(solution)/shard_map/ppermute | solution.py:41
  138.3 3.3 %collective-permute-done.17 = f32[36,18,1]{0,2,1:T(1,128)S(1)} collective-permute-done((f32[36,18,1]{0,2,1:T(1,128)S(1)}, f32[36,18,1]{0,2,1:T(1,128)S(1)}, u32[]{:S(2)}, u32[]{:S(2)}) %collective-permute-start.17) | collective-permute-done | bytes 2624 | tf_op jit(solution)/shard_map/ppermute | solution.py:41
  (89 shorter events, 37.9 us)
Async XLA Ops:
  1.6 17.8 %collective-permute-start = (f32[38,4,128]{2,1,0:T(4,128)S(1)}, f32[38,4,128]{2,1,0:T(4,128)S(1)}, u32[]{:S(2)}, u32[]{:S(2)}) collective-permute-start(f32[38,4,128]{2,1,0:T(4,128)S(1)} %slice.170), channel_id=1, source_target_pairs={{0,992},{32,0},{64,32},{96,64},{128,96},{160,128},{192,160},{224,1... | collective-permute-start | bytes 233480 | tf_op jit(solution)/shard_map/ppermute | solution.py:29
  29.3 9.6 %collective-permute-start.1 = (f32[38,128,4]{1,2,0:T(4,128)S(1)}, f32[38,128,4]{1,2,0:T(4,128)S(1)}, u32[]{:S(2)}, u32[]{:S(2)}) collective-permute-start(f32[38,128,4]{1,2,0:T(4,128)S(1)} %slice.226), channel_id=1, source_target_pairs={{0,31},{1,0},{2,1},{3,2},{4,3},{5,4},{6,5},{7,6},{8,7},{9,8},{10,9... | collective-permute-start | bytes 233480 | tf_op jit(solution)/shard_map/ppermute | solution.py:29
  48.9 4.4 %collective-permute-start.2 = (f32[36,1,64]{2,1,0:T(1,128)S(1)}, f32[36,1,64]{2,1,0:T(1,128)S(1)}, u32[]{:S(2)}, u32[]{:S(2)}) collective-permute-start(f32[36,1,64]{2,1,0:T(1,128)S(1)} %get-tuple-element.18), channel_id=1, source_target_pairs={{0,32},{32,64},{64,96},{96,128},{128,160},{160,192},{192,224},{224... | collective-permute-start | bytes 27656 | tf_op jit(solution)/shard_map/ppermute | solution.py:39
  48.9 4.4 %collective-permute-start.3 = (f32[36,1,64]{2,1,0:T(1,128)S(1)}, f32[36,1,64]{2,1,0:T(1,128)S(1)}, u32[]{:S(2)}, u32[]{:S(2)}) collective-permute-start(f32[36,1,64]{2,1,0:T(1,128)S(1)} %get-tuple-element.19), channel_id=1, source_target_pairs={{32,0},{64,32},{96,64},{128,96},{160,128},{192,160},{224,192},{256... | collective-permute-start | bytes 27656 | tf_op jit(solution)/shard_map/ppermute | solution.py:41
  51.9 23.5 %collective-permute-start.6 = (f32[38,4,64]{2,1,0:T(4,128)S(1)}, f32[38,4,64]{2,1,0:T(4,128)S(1)}, u32[]{:S(2)}, u32[]{:S(2)}) collective-permute-start(f32[38,4,64]{2,1,0:T(4,128)S(1)} %slice.244), channel_id=1, source_target_pairs={{0,992},{32,0},{64,32},{96,64},{128,96},{160,128},{192,160},{224,1... | collective-permute-start | bytes 116744 | tf_op jit(solution)/shard_map/ppermute | solution.py:29
  56.8 13.9 %collective-permute-start.4 = (f32[36,66,1]{1,2,0:T(1,128)S(1)}, f32[36,66,1]{1,2,0:T(1,128)}, u32[]{:S(2)}, u32[]{:S(2)}) collective-permute-start(f32[36,66,1]{1,2,0:T(1,128)S(1)} %copy.14), channel_id=1, source_target_pairs={{0,1},{1,2},{2,3},{3,4},{4,5},{5,6},{6,7},{7,8},{8,9},{9,10},{10,1... | collective-permute-start | bytes 28520 | tf_op jit(solution)/shard_map/ppermute | solution.py:39
  59.9 13.2 %collective-permute-start.5 = (f32[36,66,1]{1,2,0:T(1,128)}, f32[36,66,1]{1,2,0:T(1,128)}, u32[]{:S(2)}, u32[]{:S(2)}) collective-permute-start(f32[36,66,1]{1,2,0:T(1,128)} %copy.15), channel_id=1, source_target_pairs={{1,0},{2,1},{3,2},{4,3},{5,4},{6,5},{7,6},{8,7},{9,8},{10,9},{11,1... | collective-permute-start | bytes 28520 | tf_op jit(solution)/shard_map/ppermute | solution.py:41
  77.8 1.1 copy-start
  78.9 9.6 %collective-permute-start.7 = (f32[38,64,4]{1,2,0:T(4,128)S(1)}, f32[38,64,4]{1,2,0:T(4,128)S(1)}, u32[]{:S(2)}, u32[]{:S(2)}) collective-permute-start(f32[38,64,4]{1,2,0:T(4,128)S(1)} %copy.19), channel_id=1, source_target_pairs={{0,31},{1,0},{2,1},{3,2},{4,3},{5,4},{6,5},{7,6},{8,7},{9,8},{10,9... | collective-permute-start | bytes 116744 | tf_op jit(solution)/shard_map/ppermute | solution.py:29
  91.5 1.2 copy-start.2
  92.8 4.4 %collective-permute-start.8 = (f32[36,1,32]{2,1,0:T(1,128)S(1)}, f32[36,1,32]{2,1,0:T(1,128)S(1)}, u32[]{:S(2)}, u32[]{:S(2)}) collective-permute-start(f32[36,1,32]{2,1,0:T(1,128)S(1)} %get-tuple-element.22), channel_id=1, source_target_pairs={{0,32},{32,64},{64,96},{96,128},{128,160},{160,192},{192,224},{224... | collective-permute-start | bytes 13832 | tf_op jit(solution)/shard_map/ppermute | solution.py:39
  92.8 4.4 %collective-permute-start.9 = (f32[36,1,32]{2,1,0:T(1,128)S(1)}, f32[36,1,32]{2,1,0:T(1,128)S(1)}, u32[]{:S(2)}, u32[]{:S(2)}) collective-permute-start(f32[36,1,32]{2,1,0:T(1,128)S(1)} %get-tuple-element.23), channel_id=1, source_target_pairs={{32,0},{64,32},{96,64},{128,96},{160,128},{192,160},{224,192},{256... | collective-permute-start | bytes 13832 | tf_op jit(solution)/shard_map/ppermute | solution.py:41
  96.7 15.7 %collective-permute-start.12 = (f32[38,4,32]{2,1,0:T(4,128)}, f32[38,4,32]{2,1,0:T(4,128)S(1)}, u32[]{:S(2)}, u32[]{:S(2)}) collective-permute-start(f32[38,4,32]{2,1,0:T(4,128)} %slice.263), channel_id=1, source_target_pairs={{0,992},{32,0},{64,32},{96,64},{128,96},{160,128},{192,160},{224,1... | collective-permute-start | bytes 58376 | tf_op jit(solution)/shard_map/ppermute | solution.py:29
  99.7 9.7 %collective-permute-start.10 = (f32[36,34,1]{0,2,1:T(1,128)}, f32[36,34,1]{0,2,1:T(1,128)S(1)}, u32[]{:S(2)}, u32[]{:S(2)}) collective-permute-start(f32[36,34,1]{0,2,1:T(1,128)} %copy.23), channel_id=1, source_target_pairs={{0,1},{1,2},{2,3},{3,4},{4,5},{5,6},{6,7},{7,8},{8,9},{9,10},{10,1... | collective-permute-start | bytes 14696 | tf_op jit(solution)/shard_map/ppermute | solution.py:39
  102.2 9.1 %collective-permute-start.11 = (f32[36,34,1]{0,2,1:T(1,128)S(1)}, f32[36,34,1]{0,2,1:T(1,128)}, u32[]{:S(2)}, u32[]{:S(2)}) collective-permute-start(f32[36,34,1]{0,2,1:T(1,128)S(1)} %copy.24), channel_id=1, source_target_pairs={{1,0},{2,1},{3,2},{4,3},{5,4},{6,5},{7,6},{8,7},{9,8},{10,9},{11,1... | collective-permute-start | bytes 14696 | tf_op jit(solution)/shard_map/ppermute | solution.py:41
  108.3 4.1 %copy-start.1 = (f32[38,32,32]{2,1,0:T(8,128)S(1)}, f32[38,32,32]{2,1,0:T(8,128)}, u32[]{:S(2)}) copy-start(f32[38,32,32]{2,1,0:T(8,128)} %get-tuple-element.16) | copy-start | bytes 466948
  112.5 5.2 %copy-start.6 = (f32[36,1,32]{2,1,0:T(1,128)S(1)}, f32[36,1,32]{2,1,0:T(1,128)}, u32[]{:S(2)}) copy-start(f32[36,1,32]{2,1,0:T(1,128)} %copy-done.5) | copy-start | bytes 13828
  112.9 4.8 %copy-start.8 = (f32[36,1,32]{2,1,0:T(1,128)S(1)}, f32[36,1,32]{2,1,0:T(1,128)}, u32[]{:S(2)}) copy-start(f32[36,1,32]{2,1,0:T(1,128)} %copy-done.7) | copy-start | bytes 13828
  115.8 9.5 %collective-permute-start.13 = (f32[38,32,4]{0,1,2:T(8,128)S(1)}, f32[38,32,4]{0,1,2:T(8,128)S(1)}, u32[]{:S(2)}, u32[]{:S(2)}) collective-permute-start(f32[38,32,4]{0,1,2:T(8,128)S(1)} %slice.264), channel_id=1, source_target_pairs={{0,31},{1,0},{2,1},{3,2},{4,3},{5,4},{6,5},{7,6},{8,7},{9,8},{10,9... | collective-permute-start | bytes 58376 | tf_op jit(solution)/shard_map/ppermute | solution.py:29
  118.3 8.1 %copy-start.3 = (f32[36,16,16]{0,2,1:T(8,128)S(1)}, f32[36,16,16]{0,2,1:T(8,128)}, u32[]{:S(2)}) copy-start(f32[36,16,16]{0,2,1:T(8,128)} %reduce_max.19) | copy-start | bytes 110596
  126.5 4.3 %collective-permute-start.14 = (f32[36,1,16]{0,2,1:T(8,128)S(1)}, f32[36,1,16]{0,2,1:T(8,128)S(1)}, u32[]{:S(2)}, u32[]{:S(2)}) collective-permute-start(f32[36,1,16]{0,2,1:T(8,128)S(1)} %get-tuple-element.26), channel_id=1, source_target_pairs={{0,32},{32,64},{64,96},{96,128},{128,160},{160,192},{192,224},{224... | collective-permute-start | bytes 6920 | tf_op jit(solution)/shard_map/ppermute | solution.py:39
  126.5 4.3 %collective-permute-start.15 = (f32[36,1,16]{0,2,1:T(8,128)S(1)}, f32[36,1,16]{0,2,1:T(8,128)S(1)}, u32[]{:S(2)}, u32[]{:S(2)}) collective-permute-start(f32[36,1,16]{0,2,1:T(8,128)S(1)} %get-tuple-element.27), channel_id=1, source_target_pairs={{32,0},{64,32},{96,64},{128,96},{160,128},{192,160},{224,192},{256... | collective-permute-start | bytes 6920 | tf_op jit(solution)/shard_map/ppermute | solution.py:41
  130.8 7.5 %collective-permute-start.16 = (f32[36,18,1]{0,2,1:T(1,128)S(1)}, f32[36,18,1]{0,2,1:T(1,128)S(1)}, u32[]{:S(2)}, u32[]{:S(2)}) collective-permute-start(f32[36,18,1]{0,2,1:T(1,128)S(1)} %get-tuple-element.24), channel_id=1, source_target_pairs={{0,1},{1,2},{2,3},{3,4},{4,5},{5,6},{6,7},{7,8},{8,9},{9,10},{10,1... | collective-permute-start | bytes 7784 | tf_op jit(solution)/shard_map/ppermute | solution.py:39
  132.8 8.9 %collective-permute-start.17 = (f32[36,18,1]{0,2,1:T(1,128)S(1)}, f32[36,18,1]{0,2,1:T(1,128)S(1)}, u32[]{:S(2)}, u32[]{:S(2)}) collective-permute-start(f32[36,18,1]{0,2,1:T(1,128)S(1)} %get-tuple-element.25), channel_id=1, source_target_pairs={{1,0},{2,1},{3,2},{4,3},{5,4},{6,5},{7,6},{8,7},{9,8},{10,9},{11,1... | collective-permute-start | bytes 7784 | tf_op jit(solution)/shard_map/ppermute | solution.py:41
  (3 other events, 1.9 us)
where the time goes:
time: 143 us; the launch traced here: 142 us
  starting transfers between devices  49.9 us (35%)
  waiting for transfers between devices  28.1 us (20%)
  matrix products  26.5 us (19%)
  local copies, waits for them, and re-layouts  22.1 us (15%)
  other arithmetic  14.7 us (10%)
    ppermute x6, starting transfers between devices, passed_along(): lax.ppermute(x, axis, [(i, (i + by) % devices) for i in range(devices)])  23.1 us
    ppermute x6, starting transfers between devices, with_halo(): lax.ppermute(head, axis, [((i + 1) % count, i) for i in range(count)])  20.9 us
    ppermute x6, waiting for transfers between devices, passed_along(): lax.ppermute(x, axis, [(i, (i + by) % devices) for i in range(devices)])  20.1 us
    dot_general x3, matrix products, split_x(): jnp.einsum('zxy,xk->zky', values, matrix, precision=lax.Precision.HIGHEST)  14.9 us
    dot_general x3, matrix products, split_y(): jnp.dot(values.reshape(planes * length_x, length_y), matrix, precision=la...  11.6 us
    ppermute x6, starting transfers between devices, with_halo(): lax.ppermute(tail, axis, [(i, (i + 1) % count) for i in range(count)])  6.02 us
    ppermute x6, waiting for transfers between devices, with_halo(): lax.ppermute(head, axis, [((i + 1) % count, i) for i in range(count)])  4.82 us
    slice x7, local copies, waits for them, and re-layouts, with_halo(): lax.slice_in_dim(cells, cells.shape[dim] - width, cells.shape[dim], axis=...  4.54 us
  transfers between devices with their start and end apart: 18, of which 9 were waited for; matrix products, arithmetic and copies ran while one was open for 20% of the time, Pallas kernels for 0%

commit v1 on v0

v1 whole, which is shorter than its diff:
```python
import functools

import jax
import jax.numpy as jnp
from jax import lax
from jax.experimental import pallas as pl
from jax.experimental.pallas import tpu as pltpu
from jax.sharding import PartitionSpec as P

H = (
    0.3326705529509569,
    0.8068915093133388,
    0.4598775021193313,
    -0.13501102001039084,
    -0.08544127388224149,
    0.035226291882100656,
)
G = tuple((-1) ** t * H[5 - t] for t in range(6))
Z = 38
HALF = 20
BLK = 10
GRP = 3
HR = 4
CHUNKS = ((0, 10), (10, 20))
MESH = pl.DeviceIdType.MESH
roll = pltpu.roll


def lane_ids(rows):
    return lax.broadcasted_iota(jnp.int32, (rows, 128), 1)


def split(ref, lead, start, n):
    low = high = None
    for t in range(6):
        tap = ref[lead + (pl.ds(start + t, n, stride=2), slice(None))]
        low = tap * H[t] if low is None else low + tap * H[t]
        high = tap * G[t] if high is None else high + tap * G[t]
    return low, high


def pool_rows(ref, lead, start, n):
    return jnp.maximum(
        ref[lead + (pl.ds(start, n, stride=2), slice(None))],
        ref[lead + (pl.ds(start + 1, n, stride=2), slice(None))],
    )


def box_rows(ref, lead, n):
    return jnp.maximum(
        jnp.maximum(
            ref[lead + (pl.ds(7, n), slice(None))],
            ref[lead + (pl.ds(9, n), slice(None))],
        ),
        ref[lead + (pl.ds(8, n), slice(None))],
    )


def pair_of(q):
    return jnp.minimum(q + HALF, Z - 1)


def loop(lo, hi, body):
    def step(i, _):
        body(i)
        return 0

    lax.fori_loop(lo, hi, step, 0)


def kernel(
    v, o1, o2, o3,
    vb, tb, s1, d1, t2, s2, c2, pc, p1, t3, p2, c3, e1, y2, x3,
    f1y_s, f1y_r, f1x_s, f1x_r, f2x_s, f2x_r, f2y_s, f2y_r, f3y_s, f3y_r, f3x_s, f3x_r,
    in_sem, send_sem, recv_sem,
):
    nx, ny = lax.axis_size("gx"), lax.axis_size("gy")
    ix, iy = lax.axis_index("gx"), lax.axis_index("gy")
    x_prev = (lax.rem(ix + nx - 1, nx), iy)
    x_next = (lax.rem(ix + 1, nx), iy)
    y_prev = (ix, lax.rem(iy + ny - 1, ny))
    y_next = (ix, lax.rem(iy + 1, ny))
    counter = [0]

    def remote(src, dst, target):
        k = counter[0]
        counter[0] += 1
        return pltpu.make_async_remote_copy(
            src_ref=src, dst_ref=dst, send_sem=send_sem.at[k], recv_sem=recv_sem.at[k],
            device_id=target, device_id_type=MESH,
        )

    def frames(send, recv, prev, following):
        return [
            remote(send.at[0], recv.at[1], prev),
            remote(send.at[1], recv.at[0], following),
        ]

    spans = []
    for q0, q1 in CHUNKS:
        spans.append(((q0, q1), (q0 + HALF, min(q1 + HALF, Z))))
    loads, hx1, hy1 = [], [], []
    for number, pieces in enumerate(spans):
        row = []
        for part, (a, b) in enumerate(pieces):
            row.append(
                pltpu.make_async_copy(
                    v.at[pl.ds(a, b - a)], vb.at[pl.ds(a, b - a), pl.ds(0, 128)],
                    in_sem.at[2 * number + part],
                )
            )
        loads.append(row)
    for row in loads:
        for copy in row:
            copy.start()

    barrier = pltpu.get_barrier_semaphore()
    for device in (x_prev, x_next, y_prev, y_next):
        pl.semaphore_signal(barrier, inc=1, device_id=device, device_id_type=MESH)
    pl.semaphore_wait(barrier, 4)

    for pieces in spans:
        row = [
            remote(
                v.at[pl.ds(a, b - a), pl.ds(0, HR)],
                vb.at[pl.ds(a, b - a), pl.ds(128, HR)], x_prev,
            )
            for a, b in pieces
        ]
        for copy in row:
            copy.start()
        hx1.append(row)

    def stage_x1(p):
        lows, highs = [], []
        for piece in range(2):
            low, high = split(vb, (p,), 64 * piece, 32)
            lows.append(low)
            highs.append(high)
        tb[p, pl.ds(0, 128), :] = jnp.concatenate(lows + highs, axis=0).T

    for number, pieces in enumerate(spans):
        for copy in loads[number]:
            copy.wait()
        for copy in hx1[number]:
            copy.wait_recv()
        for a, b in pieces:
            loop(a, b, stage_x1)
        row = [
            remote(
                tb.at[pl.ds(a, b - a), pl.ds(0, HR)],
                tb.at[pl.ds(a, b - a), pl.ds(128, HR)], y_prev,
            )
            for a, b in pieces
        ]
        for copy in row:
            copy.start()
        hy1.append(row)

    first = lane_ids(32) < 64

    def stage_y1(q):
        other = pair_of(q)
        for piece in range(2):
            low_a, high_a = split(tb, (q,), 64 * piece, 32)
            low_b, high_b = split(tb, (other,), 64 * piece, 32)
            turned_a, turned_b = roll(low_a, 64, 1), roll(low_b, 64, 1)
            s1[q, pl.ds(32 * piece, 32), :] = jnp.where(first, low_a, turned_b)
            cross = jnp.abs(jnp.where(first, turned_a, low_b))
            high_a, high_b = jnp.abs(high_a), jnp.abs(high_b)
            high_a = jnp.maximum(high_a, roll(high_a, 64, 1))
            high_b = jnp.maximum(high_b, roll(high_b, 64, 1))
            detail = jnp.maximum(jnp.where(first, high_a, high_b), cross)
            d1[q, pl.ds(8 + 32 * piece, 32), :] = detail
            if piece == 0:
                f1y_s[0, q, :, :] = detail[0:1]
            else:
                f1y_s[1, q, :, :] = detail[31:32]

    hy2 = []
    for number, (q0, q1) in enumerate(CHUNKS):
        for copy in hy1[number]:
            copy.wait_recv()
        loop(q0, q1, stage_y1)
        copy = remote(
            s1.at[pl.ds(q0, q1 - q0), pl.ds(0, HR)],
            s1.at[pl.ds(q0, q1 - q0), pl.ds(64, HR)], y_prev,
        )
        copy.start()
        hy2.append(copy)
    f1y = frames(f1y_s, f1y_r, y_prev, y_next)
    for copy in f1y:
        copy.start()

    quarter = lax.rem(lane_ids(32), 64) < 32

    def stage_p1(b):
        rows = [pool_rows(d1, (b + 5 * k,), 8, 32) for k in range(4)]
        p1[b, :, :] = jnp.concatenate(rows, axis=0).T
        pool_a = pool_rows(p1, (b,), 0, 32)
        pool_b = pool_rows(p1, (b,), 64, 32)
        pc[b, :, :] = jnp.where(quarter, pool_a, roll(pool_b, 32, 1))
        pc[b + 5, :, :] = jnp.where(quarter, roll(pool_a, 96, 1), pool_b)

    loop(0, 5, stage_p1)

    def stage_y2(b):
        rows = []
        for q in (b, b + BLK):
            rows += split(s1, (q,), 0, 32)
        turned = jnp.concatenate(rows, axis=0).T
        t2[b, 0, pl.ds(0, 64), :] = turned[:64]
        t2[b, 1, pl.ds(0, 64), :] = turned[64:]

    for copy in hy2:
        copy.wait_recv()
    loop(0, BLK, stage_y2)
    hx2 = remote(
        t2.at[:, :, pl.ds(0, HR)], t2.at[:, :, pl.ds(64, HR)], x_prev
    )
    hx2.start()

    for copy in f1y:
        copy.wait_recv()

    def stage_l1y(b):
        rows = []
        for q in (b, b + BLK):
            d1[q, 7:8, :] = f1y_r[0, q, :, :]
            d1[q, 72:73, :] = f1y_r[1, q, :, :]
            rows.append(box_rows(d1, (q,), 64))
        turned = jnp.concatenate(rows, axis=0).T
        for k in range(2):
            e1[b, k, pl.ds(8, 64), :] = turned[64 * k : 64 * k + 64]
            f1x_s[0, b, k, :, :] = turned[64 * k : 64 * k + 1]
            f1x_s[1, b, k, :, :] = turned[64 * k + 63 : 64 * k + 64]

    loop(0, BLK, stage_l1y)
    f1x = frames(f1x_s, f1x_r, x_prev, x_next)
    for copy in f1x:
        copy.start()

    def stage_x2(b):
        lows, details = [], []
        for k in range(2):
            low, high = split(t2, (b, k), 0, 32)
            high = jnp.abs(high)
            lows.append(low)
            details.append(
                jnp.maximum(high, roll(jnp.maximum(jnp.abs(low), high), 96, 1))
            )
        s2[b, pl.ds(0, 32), :] = jnp.where(quarter, lows[0], roll(lows[1], 32, 1))
        detail = jnp.where(quarter, details[0], roll(details[1], 32, 1))
        detail = jnp.maximum(detail, pc[b, :, :])
        c2[b, pl.ds(8, 32), :] = detail
        f2x_s[0, b, :, :] = detail[0:1]
        f2x_s[1, b, :, :] = detail[31:32]

    hx2.wait_recv()
    loop(0, BLK, stage_x2)
    hx3 = remote(s2.at[:, pl.ds(0, HR)], s2.at[:, pl.ds(32, HR)], x_prev)
    hx3.start()
    f2x = frames(f2x_s, f2x_r, x_prev, x_next)
    for copy in f2x:
        copy.start()

    def blocks_of(c):
        return [jnp.minimum(4 * c + k, BLK - 1) for k in range(4)]

    def stage_p2(c):
        rows = []
        for b in blocks_of(c):
            pooled = pool_rows(c2, (b,), 8, 16)
            rows += [pooled, pooled]
        p2[c, :, :] = jnp.concatenate(rows, axis=0).T

    loop(0, GRP, stage_p2)

    for copy in f1x:
        copy.wait_recv()

    def stage_l1x(b):
        for k in range(2):
            e1[b, k, 7:8, :] = f1x_r[0, b, k, :, :]
            e1[b, k, 72:73, :] = f1x_r[1, b, k, :, :]
            boxed = box_rows(e1, (b, k), 64)
            o1[b + HALF * k, :, :] = boxed[:, :64]
            o1[b + HALF * k + BLK, :, :] = roll(boxed, 64, 1)[:, :64]

    def stage_x3(c):
        rows = []
        for b in blocks_of(c):
            rows += split(s2, (b,), 0, 16)
        turned = jnp.concatenate(rows, axis=0).T
        for g in range(4):
            t3[c, g, pl.ds(0, 32), :] = turned[32 * g : 32 * g + 32]

    hx3.wait_recv()
    loop(0, GRP, stage_x3)
    hy3 = remote(
        t3.at[:, :, pl.ds(0, HR)], t3.at[:, :, pl.ds(32, HR)], y_prev
    )
    hy3.start()

    loop(0, BLK // 2, stage_l1x)

    for copy in f2x:
        copy.wait_recv()

    def stage_l2x(c):
        rows = []
        for b in blocks_of(c):
            c2[b, 7:8, :] = f2x_r[0, b, :, :]
            c2[b, 40:41, :] = f2x_r[1, b, :, :]
            rows.append(box_rows(c2, (b,), 32))
        turned = jnp.concatenate(rows, axis=0).T
        for g in range(4):
            y2[c, g, pl.ds(8, 32), :] = turned[32 * g : 32 * g + 32]
            f2y_s[0, c, g, :, :] = turned[32 * g : 32 * g + 1]
            f2y_s[1, c, g, :, :] = turned[32 * g + 31 : 32 * g + 32]

    loop(0, GRP, stage_l2x)
    f2y = frames(f2y_s, f2y_r, y_prev, y_next)
    for copy in f2y:
        copy.start()

    def stage_y3(c):
        for g in range(4):
            low, high = split(t3, (c, g), 0, 16)
            high = jnp.abs(high)
            detail = jnp.maximum(high, roll(jnp.maximum(jnp.abs(low), high), 112, 1))
            detail = jnp.maximum(detail, pool_rows(p2, (c,), 32 * g, 16))
            c3[c, g, pl.ds(8, 16), :] = detail
            f3y_s[0, c, g, :, :] = detail[0:1]
            f3y_s[1, c, g, :, :] = detail[15:16]

    hy3.wait_recv()
    loop(0, GRP, stage_y3)
    f3y = frames(f3y_s, f3y_r, y_prev, y_next)
    for copy in f3y:
        copy.start()

    loop(BLK // 2, BLK, stage_l1x)

    for copy in f3y:
        copy.wait_recv()

    def stage_l3y(c):
        rows = []
        for g in range(4):
            c3[c, g, 7:8, :] = f3y_r[0, c, g, :, :]
            c3[c, g, 24:25, :] = f3y_r[1, c, g, :, :]
            rows.append(box_rows(c3, (c, g), 16))
        turned = jnp.concatenate(rows + rows, axis=0).T
        for k in range(4):
            x3[c, k, pl.ds(8, 16), :] = turned[32 * k : 32 * k + 16]
            f3x_s[0, c, k, :, :] = turned[32 * k : 32 * k + 1]
            f3x_s[1, c, k, :, :] = turned[32 * k + 15 : 32 * k + 16]

    loop(0, GRP, stage_l3y)
    f3x = frames(f3x_s, f3x_r, x_prev, x_next)
    for copy in f3x:
        copy.start()

    for copy in f2y:
        copy.wait_recv()

    offsets = (0, HALF, BLK, HALF + BLK)
    for c in range(GRP):
        rows = []
        for g in range(4):
            y2[c, g, 7:8, :] = f2y_r[0, c, g, :, :]
            y2[c, g, 40:41, :] = f2y_r[1, c, g, :, :]
            rows.append(box_rows(y2, (c, g), 32))
        turned = jnp.concatenate(rows, axis=0).T
        for k in range(min(4, BLK - 4 * c)):
            block = turned[32 * k : 32 * k + 32]
            for g in range(4):
                spun = roll(block, 128 - 32 * g, 1) if g else block
                o2[4 * c + k + offsets[g], :, :] = spun[:, :32]

    for copy in f3x:
        copy.wait_recv()
    for c in range(GRP):
        for k in range(min(4, BLK - 4 * c)):
            x3[c, k, 7:8, :] = f3x_r[0, c, k, :, :]
            x3[c, k, 24:25, :] = f3x_r[1, c, k, :, :]
            block = box_rows(x3, (c, k), 16)
            for g in range(4):
                spun = roll(block, 128 - 16 * g, 1) if g else block
                o3[4 * c + k + offsets[g], :, :] = spun[:, :16]

    for row in hx1 + hy1 + [hy2, f1y, [hx2], f1x, [hx3], f2x, [hy3], f2y, f3y, f3x]:
        for copy in row:
            copy.wait_send()


def deepest(values):
    count = Z - 2
    return jnp.maximum(
        jnp.maximum(values[:count], values[1 : count + 1]), values[2 : count + 2]
    )


def shards(vorticity):
    f32 = jnp.float32
    copies = 4 * len(CHUNKS) + len(CHUNKS) + 4 + 12
    rows = lambda *shape: pltpu.VMEM(shape, f32)
    frame = lambda *shape: [pltpu.VMEM((2,) + shape + (1, 128), f32)] * 2
    planes = 2 * HALF
    o1, o2, o3 = pl.pallas_call(
        kernel,
        out_shape=[
            jax.ShapeDtypeStruct((planes, 64, 64), f32),
            jax.ShapeDtypeStruct((planes, 32, 32), f32),
            jax.ShapeDtypeStruct((planes, 16, 16), f32),
        ],
        in_specs=[pl.BlockSpec(memory_space=pl.ANY)],
        out_specs=[pl.BlockSpec(memory_space=pltpu.VMEM)] * 3,
        scratch_shapes=[
            rows(Z, 136, 128),
            rows(Z, 136, 128),
            rows(HALF, 72, 128),
            rows(HALF, 80, 128),
            rows(BLK, 2, 72, 128),
            rows(BLK, 40, 128),
            rows(BLK, 48, 128),
            rows(BLK, 32, 128),
            rows(5, 128, 128),
            rows(GRP, 4, 40, 128),
            rows(GRP, 128, 128),
            rows(GRP, 4, 32, 128),
            rows(BLK, 2, 80, 128),
            rows(GRP, 4, 48, 128),
            rows(GRP, 4, 32, 128),
            *frame(HALF),
            *frame(BLK, 2),
            *frame(BLK),
            *frame(GRP, 4),
            *frame(GRP, 4),
            *frame(GRP, 4),
            pltpu.SemaphoreType.DMA((2 * len(CHUNKS),)),
            pltpu.SemaphoreType.DMA((copies,)),
            pltpu.SemaphoreType.DMA((copies,)),
        ],
        compiler_params=pltpu.CompilerParams(
            collective_id=0, has_side_effects=True, vmem_limit_bytes=40 * 2**20
        ),
    )(vorticity)
    return deepest(o1), deepest(o2), deepest(o3)


def solution(mesh):
    placed = P(None, "gx", "gy")
    return jax.shard_map(
        shards, mesh=mesh, in_specs=(placed,), out_specs=(placed,) * 3, check_vma=False
    )
```

time: 143 us -> 55.5 us (0.39)
  the two profiles are of different devices: /device:TPU:62 before, /device:TPU:1 now
where the time goes in v1:
time: 55.5 us; the launch traced here: 55.3 us
  Pallas kernels  49.6 us (89%)
  local copies, waits for them, and re-layouts  3.79 us (7%)
  other arithmetic  1.3 us (2%)
  between operations  0.66 us (1%)
    pallas_call x1, Pallas kernels, shards(): pl.pallas_call(kernel, out_shape=[jax.ShapeDtypeStruct((planes, 64, 64),...  49.6 us
    unnamed x4, local copies, waits for them, and re-layouts  3.79 us
    max x3, other arithmetic, deepest(): jnp.maximum(jnp.maximum(values[:count], values[1:count + 1]), values[2:co...  1.3 us

profile of v1, /device:TPU:1, one launch (start us, length us, event | category | flops | bytes accessed | tf_op | source)
XLA Modules:
  0.0 55.3 jit_solution(936971060897463246)
XLA Ops:
  0.6 0.0 copy-start
  0.6 1.7 %copy-done = f32[38,128,128]{2,1,0:T(8,128)S(1)} copy-done((f32[38,128,128]{2,1,0:T(8,128)S(1)}, f32[38,128,128]{2,1,0:T(8,128)}, u32[]{:S(2)}) %copy-start) | copy-done | bytes 2490392
  2.3 49.6 %shard_map.38 = (f32[40,64,64]{2,1,0:T(8,128)S(1)}, f32[40,32,32]{2,1,0:T(8,128)S(1)}, f32[40,16,16]{2,1,0:T(8,128)S(1)}) custom-call(f32[38,128,128]{2,1,0:T(8,128)S(1)} %copy-done), custom_call_target="tpu_custom_call" | custom-call | tf_op jit(solution)/shard_map/pallas_call | solution.py:411
  51.9 1.2 %slice_maximum_fusion = f32[36,64,64]{2,1,0:T(8,128)} fusion(f32[40,64,64]{2,1,0:T(8,128)S(1)} %get-tuple-element.6), kind=kLoop, calls=%fused_computation | loop fusion | flops 294912 | bytes 2359296 | tf_op jit(solution)/shard_map/max | solution.py:400
  53.2 0.9 %copy.5 = f32[36,16,16]{0,2,1:T(8,128)} copy(f32[36,16,16]{2,1,0:T(8,128)S(1)} %slice_maximum_fusion.2) | data formatting | bytes 73728
  54.0 0.1 slice_maximum_fusion.1
  54.1 1.2 %copy.4 = f32[36,32,32]{0,2,1:T(8,128)} copy(f32[36,32,32]{2,1,0:T(8,128)S(1)} %slice_maximum_fusion.1) | data formatting | bytes 294912
  (1 shorter events, 0.0 us)
Async XLA Ops:
  0.6 1.7 %copy-start = (f32[38,128,128]{2,1,0:T(8,128)S(1)}, f32[38,128,128]{2,1,0:T(8,128)}, u32[]{:S(2)}) copy-start(f32[38,128,128]{2,1,0:T(8,128)} %v.1) | copy-start | bytes 7471108

commit v2 on v1

--- a/solution.py
+++ b/solution.py
@@ -21,6 +21,9 @@
 BLK = 10
 GRP = 3
 HR = 4
+OUT = Z - 2
+PITCH = 48
+UNROLL = 5
 CHUNKS = ((0, 10), (10, 20))
 MESH = pl.DeviceIdType.MESH
 roll = pltpu.roll
@@ -65,12 +68,12 @@
         body(i)
         return 0
 
-    lax.fori_loop(lo, hi, step, 0)
+    lax.fori_loop(lo, hi, step, 0, unroll=min(UNROLL, hi - lo))
 
 
 def kernel(
     v, o1, o2, o3,
-    vb, tb, s1, d1, t2, s2, c2, pc, p1, t3, p2, c3, e1, y2, x3,
+    vb, tb, s1, d1, t2, s2, c2, pc, p1, t3, p2, c3, e1, eb, y2, w2, x3, w3,
     f1y_s, f1y_r, f1x_s, f1x_r, f2x_s, f2x_r, f2y_s, f2y_r, f3y_s, f3y_r, f3x_s, f3x_r,
     in_sem, send_sem, recv_sem,
 ):
@@ -283,9 +286,29 @@
         for k in range(2):
             e1[b, k, 7:8, :] = f1x_r[0, b, k, :, :]
             e1[b, k, 72:73, :] = f1x_r[1, b, k, :, :]
-            boxed = box_rows(e1, (b, k), 64)
-            o1[b + HALF * k, :, :] = boxed[:, :64]
-            o1[b + HALF * k + BLK, :, :] = roll(boxed, 64, 1)[:, :64]
+            eb[b, k, :, :] = box_rows(e1, (b, k), 64)
+
+    def deep(b, k):
+        return jnp.maximum(jnp.maximum(eb[b, k], eb[b + 1, k]), eb[b + 2, k])
+
+    def stage_o1(b):
+        for k in range(2):
+            deepest = deep(b, k)
+            o1[b + HALF * k, :, :] = deepest[:, :64]
+            if k == 0:
+                o1[b + BLK, :, :] = roll(deepest, 64, 1)[:, :64]
+
+    def stage_o1_rest(b):
+        o1[b + HALF + BLK, :, :] = roll(deep(b, 1), 64, 1)[:, :64]
+
+    def finish_l1():
+        half = lane_ids(64) < 64
+        for b in range(2):
+            later = roll(eb[b, 1], 64, 1)
+            eb[BLK + b, 0] = jnp.where(half, roll(eb[b, 0], 64, 1), later)
+            eb[BLK + b, 1] = later
+        loop(0, BLK, stage_o1)
+        loop(0, OUT - HALF - BLK, stage_o1_rest)
 
     def stage_x3(c):
         rows = []
@@ -341,6 +364,7 @@
         copy.start()
 
     loop(BLK // 2, BLK, stage_l1x)
+    finish_l1()
 
     for copy in f3y:
         copy.wait_recv()
@@ -377,7 +401,19 @@
             block = turned[32 * k : 32 * k + 32]
             for g in range(4):
                 spun = roll(block, 128 - 32 * g, 1) if g else block
-                o2[4 * c + k + offsets[g], :, :] = spun[:, :32]
+                w2[pl.ds(4 * c + k + offsets[g], 32, stride=PITCH), :] = spun
+
+    def planes_last(w, x, n):
+        start = pl.multiple_of(x * PITCH, 8)
+        deepest = w[pl.ds(start, 40), :]
+        for shift in (1, 2):
+            deepest = jnp.maximum(deepest, w[pl.ds(start + shift, 40), :])
+        return deepest.T[:n, :OUT]
+
+    def stage_o2(x):
+        o2[x, :, :] = planes_last(w2, x, 32)
+
+    loop(0, 32, stage_o2)
 
     for copy in f3x:
         copy.wait_recv()
@@ -388,18 +424,16 @@
             block = box_rows(x3, (c, k), 16)
             for g in range(4):
                 spun = roll(block, 128 - 16 * g, 1) if g else block
-                o3[4 * c + k + offsets[g], :, :] = spun[:, :16]
+                w3[pl.ds(4 * c + k + offsets[g], 16, stride=PITCH), :] = spun
+
+    def stage_o3(x):
+        o3[x, :, :] = planes_last(w3, x, 16)
+
+    loop(0, 16, stage_o3)
 
     for row in hx1 + hy1 + [hy2, f1y, [hx2], f1x, [hx3], f2x, [hy3], f2y, f3y, f3x]:
         for copy in row:
             copy.wait_send()
-
-
-def deepest(values):
-    count = Z - 2
-    return jnp.maximum(
-        jnp.maximum(values[:count], values[1 : count + 1]), values[2 : count + 2]
-    )
 
 
 def shards(vorticity):
@@ -407,15 +441,14 @@
     copies = 4 * len(CHUNKS) + len(CHUNKS) + 4 + 12
     rows = lambda *shape: pltpu.VMEM(shape, f32)
     frame = lambda *shape: [pltpu.VMEM((2,) + shape + (1, 128), f32)] * 2
-    planes = 2 * HALF
     o1, o2, o3 = pl.pallas_call(
         kernel,
         out_shape=[
-            jax.ShapeDtypeStruct((planes, 64, 64), f32),
-            jax.ShapeDtypeStruct((planes, 32, 32), f32),
-            jax.ShapeDtypeStruct((planes, 16, 16), f32),
+            jax.ShapeDtypeStruct((OUT, 64, 64), f32),
+            jax.ShapeDtypeStruct((32, 32, OUT), f32),
+            jax.ShapeDtypeStruct((16, 16, OUT), f32),
         ],
-        in_specs=[pl.BlockSpec(memory_space=pl.ANY)],
+        in_specs=[pl.BlockSpec(memory_space=pltpu.HBM)],
         out_specs=[pl.BlockSpec(memory_space=pltpu.VMEM)] * 3,
         scratch_shapes=[
             rows(Z, 136, 128),
@@ -431,8 +464,11 @@
             rows(GRP, 128, 128),
             rows(GRP, 4, 32, 128),
             rows(BLK, 2, 80, 128),
+            rows(BLK + 2, 2, 64, 128),
             rows(GRP, 4, 48, 128),
+            rows(32 * PITCH, 128),
             rows(GRP, 4, 32, 128),
+            rows(16 * PITCH, 128),
             *frame(HALF),
             *frame(BLK, 2),
             *frame(BLK),
@@ -444,10 +480,10 @@
             pltpu.SemaphoreType.DMA((copies,)),
         ],
         compiler_params=pltpu.CompilerParams(
-            collective_id=0, has_side_effects=True, vmem_limit_bytes=40 * 2**20
+            collective_id=0, has_side_effects=True, vmem_limit_bytes=51 * 2**20
         ),
     )(vorticity)
-    return deepest(o1), deepest(o2), deepest(o3)
+    return o1, jnp.transpose(o2, (2, 0, 1)), jnp.transpose(o3, (2, 0, 1))
 
 
 def solution(mesh):

time: 55.5 us -> 49.2 us (0.89)
  Pallas kernels: 49.6 us -> 45.9 us
  local copies, waits for them, and re-layouts: 3.79 us -> 2.46 us
  other arithmetic: 1.3 us -> 0 us
    pallas_call x1, Pallas kernels: 49.6 us -> 45.9 us  [shards(): pl.pallas_call(kernel, out_shape=[jax.ShapeDtypeStruct((OUT, 64, 64), f32...]
    unnamed x4 -> x3, local copies, waits for them, and re-layouts: 3.79 us -> 2.46 us
    max x3 -> x0, other arithmetic: 1.3 us -> none  [deepest(): jnp.maximum(jnp.maximum(values[:count], values[1:count + 1]), values[2:co...]
where the time goes in v2:
time: 49.2 us; the launch traced here: 49 us
  Pallas kernels  45.9 us (93%)
  local copies, waits for them, and re-layouts  2.46 us (5%)
  between operations  0.64 us (1%)
    pallas_call x1, Pallas kernels, shards(): pl.pallas_call(kernel, out_shape=[jax.ShapeDtypeStruct((OUT, 64, 64), f32...  45.9 us
    unnamed x3, local copies, waits for them, and re-layouts  2.46 us

profile of v2, /device:TPU:1, one launch (start us, length us, event | category | flops | bytes accessed | tf_op | source)
XLA Modules:
  0.0 49.0 jit_solution(17750801825668958649)
XLA Ops:
  0.6 45.9 %shard_map.38 = (f32[36,64,64]{2,1,0:T(8,128)S(1)}, f32[32,32,36]{2,1,0:T(8,128)S(1)}, f32[16,16,36]{2,1,0:T(8,128)S(1)}) custom-call(f32[38,128,128]{2,1,0:T(8,128)} %v.1), custom_call_target="tpu_custom_call" | custom-call | tf_op jit(solution)/shard_map/pallas_call | solution.py:444
  46.6 1.0 %copy.7 = f32[36,64,64]{2,1,0:T(8,128)} copy(f32[36,64,64]{2,1,0:T(8,128)S(1)} %get-tuple-element.12) | data formatting | bytes 1179648
  47.6 0.8 %copy.8 = f32[36,32,32]{0,2,1:T(8,128)} copy(f32[36,32,32]{0,2,1:T(8,128)S(1)} %bitcast.2) | data formatting | bytes 294912
  48.4 0.7 %copy.9 = f32[36,16,16]{0,2,1:T(8,128)} copy(f32[36,16,16]{0,2,1:T(8,128)S(1)} %bitcast.3) | data formatting | bytes 73728

commit v3 on v2

--- a/solution.py
+++ b/solution.py
@@ -19,7 +19,8 @@
 Z = 38
 HALF = 20
 BLK = 10
-GRP = 3
+QUAD = 3
+TWO = 5
 HR = 4
 OUT = Z - 2
 PITCH = 48
@@ -73,8 +74,8 @@
 
 def kernel(
     v, o1, o2, o3,
-    vb, tb, s1, d1, t2, s2, c2, pc, p1, t3, p2, c3, e1, eb, y2, w2, x3, w3,
-    f1y_s, f1y_r, f1x_s, f1x_r, f2x_s, f2x_r, f2y_s, f2y_r, f3y_s, f3y_r, f3x_s, f3x_r,
+    vb, tb, s1, d1, t2, s2, c2, pc, p1, t3, p2, p3, c3, e1, eb, y2, w2, x3, w3,
+    lk_s, lk_r, lh, f1y_s, f1y_r, f1x_s, f1x_r, fp_s, fp_r, f2y_s, f2y_r, f3p_s, f3p_r, t3_s, t3_r,
     in_sem, send_sem, recv_sem,
 ):
     nx, ny = lax.axis_size("gx"), lax.axis_size("gy")
@@ -142,6 +143,13 @@
             highs.append(high)
         tb[p, pl.ds(0, 128), :] = jnp.concatenate(lows + highs, axis=0).T
 
+    def both(ref, q, start, n):
+        later = roll(ref[pair_of(q), pl.ds(start, n), :], 64, 1)
+        return jnp.where(lane_ids(n) < 64, ref[q, pl.ds(start, n), :], later)
+
+    def stage_k1(q):
+        lk_s[q, :, :] = both(tb, q, HR, 8)
+
     for number, pieces in enumerate(spans):
         for copy in loads[number]:
             copy.wait()
@@ -158,7 +166,11 @@
         ]
         for copy in row:
             copy.start()
-        hy1.append(row)
+        q0, q1 = CHUNKS[number]
+        loop(q0, q1, stage_k1)
+        copy = remote(lk_s.at[pl.ds(q0, q1 - q0)], lk_r.at[pl.ds(q0, q1 - q0)], y_prev)
+        copy.start()
+        hy1.append(row + [copy])
 
     first = lane_ids(32) < 64
 
@@ -180,17 +192,20 @@
             else:
                 f1y_s[1, q, :, :] = detail[31:32]
 
-    hy2 = []
+    def stage_k2(q):
+        lh[q, pl.ds(0, HR), :] = both(tb, q, 128, HR)
+        lh[q, pl.ds(HR, 8), :] = lk_r[q, :, :]
+        low = None
+        for t in range(6):
+            tap = lh[q, pl.ds(t, HR, stride=2), :] * H[t]
+            low = tap if low is None else low + tap
+        s1[q, pl.ds(64, HR), :] = low
+
     for number, (q0, q1) in enumerate(CHUNKS):
         for copy in hy1[number]:
             copy.wait_recv()
         loop(q0, q1, stage_y1)
-        copy = remote(
-            s1.at[pl.ds(q0, q1 - q0), pl.ds(0, HR)],
-            s1.at[pl.ds(q0, q1 - q0), pl.ds(64, HR)], y_prev,
-        )
-        copy.start()
-        hy2.append(copy)
+        loop(q0, q1, stage_k2)
     f1y = frames(f1y_s, f1y_r, y_prev, y_next)
     for copy in f1y:
         copy.start()
@@ -202,26 +217,33 @@
         p1[b, :, :] = jnp.concatenate(rows, axis=0).T
         pool_a = pool_rows(p1, (b,), 0, 32)
         pool_b = pool_rows(p1, (b,), 64, 32)
-        pc[b, :, :] = jnp.where(quarter, pool_a, roll(pool_b, 32, 1))
-        pc[b + 5, :, :] = jnp.where(quarter, roll(pool_a, 96, 1), pool_b)
-
-    loop(0, 5, stage_p1)
+        for block, pooled in (
+            (b, jnp.where(quarter, pool_a, roll(pool_b, 32, 1))),
+            (b + 5, jnp.where(quarter, roll(pool_a, 96, 1), pool_b)),
+        ):
+            pc[block, pl.ds(8, 32), :] = pooled
+            fp_s[0, block, :, :] = pooled[0:2]
+            fp_s[1, block, :, :] = pooled[30:32]
 
     def stage_y2(b):
         rows = []
         for q in (b, b + BLK):
             rows += split(s1, (q,), 0, 32)
         turned = jnp.concatenate(rows, axis=0).T
-        t2[b, 0, pl.ds(0, 64), :] = turned[:64]
-        t2[b, 1, pl.ds(0, 64), :] = turned[64:]
-
-    for copy in hy2:
-        copy.wait_recv()
+        t2[b, 0, pl.ds(8, 64), :] = turned[:64]
+        t2[b, 1, pl.ds(8, 64), :] = turned[64:]
+
     loop(0, BLK, stage_y2)
-    hx2 = remote(
-        t2.at[:, :, pl.ds(0, HR)], t2.at[:, :, pl.ds(64, HR)], x_prev
-    )
-    hx2.start()
+    hx2 = [
+        remote(t2.at[:, :, pl.ds(8, 16)], t2.at[:, :, pl.ds(72, 16)], x_prev),
+        remote(t2.at[:, :, pl.ds(64, 8)], t2.at[:, :, pl.ds(0, 8)], x_next),
+    ]
+    for copy in hx2:
+        copy.start()
+    loop(0, 5, stage_p1)
+    fp = frames(fp_s, fp_r, x_prev, x_next)
+    for copy in fp:
+        copy.start()
 
     for copy in f1y:
         copy.wait_recv()
@@ -243,41 +265,75 @@
     for copy in f1x:
         copy.start()
 
+    wide = lax.rem(lane_ids(40), 64) < 32
+
     def stage_x2(b):
+        pc[b, 6:8, :] = fp_r[0, b, :, :]
+        pc[b, 40:42, :] = fp_r[1, b, :, :]
         lows, details = [], []
         for k in range(2):
-            low, high = split(t2, (b, k), 0, 32)
+            low, high = split(t2, (b, k), 4, 40)
             high = jnp.abs(high)
             lows.append(low)
             details.append(
                 jnp.maximum(high, roll(jnp.maximum(jnp.abs(low), high), 96, 1))
             )
-        s2[b, pl.ds(0, 32), :] = jnp.where(quarter, lows[0], roll(lows[1], 32, 1))
-        detail = jnp.where(quarter, details[0], roll(details[1], 32, 1))
-        detail = jnp.maximum(detail, pc[b, :, :])
-        c2[b, pl.ds(8, 32), :] = detail
-        f2x_s[0, b, :, :] = detail[0:1]
-        f2x_s[1, b, :, :] = detail[31:32]
-
-    hx2.wait_recv()
+        s2[b, pl.ds(0, 40), :] = jnp.where(wide, lows[0], roll(lows[1], 32, 1))
+        detail = jnp.where(wide, details[0], roll(details[1], 32, 1))
+        c2[b, pl.ds(6, 40), :] = jnp.maximum(detail, pc[b, pl.ds(6, 40), :])
+
+    for copy in hx2 + fp:
+        copy.wait_recv()
     loop(0, BLK, stage_x2)
-    hx3 = remote(s2.at[:, pl.ds(0, HR)], s2.at[:, pl.ds(32, HR)], x_prev)
-    hx3.start()
-    f2x = frames(f2x_s, f2x_r, x_prev, x_next)
-    for copy in f2x:
-        copy.start()
-
-    def blocks_of(c):
-        return [jnp.minimum(4 * c + k, BLK - 1) for k in range(4)]
+
+    def stage_x3(c):
+        rows = []
+        for k in range(2):
+            low, high = split(s2, (2 * c + k,), 0, 24)
+            rows += [low, high, low[:16]]
+        turned = jnp.concatenate(rows, axis=0).T
+        for g in range(4):
+            piece = turned[32 * g : 32 * g + 32]
+            t3[c, g, pl.ds(8, 32), :] = piece
+            t3_s[c, g, :, :] = piece[30:32]
+
+    loop(0, TWO, stage_x3)
+    hy3 = [
+        remote(t3.at[:, :, pl.ds(8, 6)], t3.at[:, :, pl.ds(40, 6)], y_prev),
+        remote(t3_s, t3_r, y_next),
+    ]
+    for copy in hy3:
+        copy.start()
 
     def stage_p2(c):
         rows = []
-        for b in blocks_of(c):
-            pooled = pool_rows(c2, (b,), 8, 16)
-            rows += [pooled, pooled]
+        for k in range(2):
+            pooled = pool_rows(c2, (2 * c + k,), 6, 24)
+            rows += [pooled, pooled, pooled[:16]]
         p2[c, :, :] = jnp.concatenate(rows, axis=0).T
-
-    loop(0, GRP, stage_p2)
+        for g in range(4):
+            pooled = pool_rows(p2, (c,), 32 * g, 16)
+            p3[c, g, pl.ds(8, 16), :] = pooled
+            f3p_s[0, c, g, :, :] = pooled[0:1]
+            f3p_s[1, c, g, :, :] = pooled[15:16]
+
+    loop(0, TWO, stage_p2)
+    f3p = frames(f3p_s, f3p_r, y_prev, y_next)
+    for copy in f3p:
+        copy.start()
+
+    def stage_l2x(c):
+        rows = [box_rows(c2, (jnp.minimum(4 * c + k, BLK - 1),), 32) for k in range(4)]
+        turned = jnp.concatenate(rows, axis=0).T
+        for g in range(4):
+            y2[c, g, pl.ds(8, 32), :] = turned[32 * g : 32 * g + 32]
+            f2y_s[0, c, g, :, :] = turned[32 * g : 32 * g + 1]
+            f2y_s[1, c, g, :, :] = turned[32 * g + 31 : 32 * g + 32]
+
+    loop(0, QUAD, stage_l2x)
+    f2y = frames(f2y_s, f2y_r, y_prev, y_next)
+    for copy in f2y:
+        copy.start()
 
     for copy in f1x:
         copy.wait_recv()
@@ -310,87 +366,32 @@
         loop(0, BLK, stage_o1)
         loop(0, OUT - HALF - BLK, stage_o1_rest)
 
-    def stage_x3(c):
-        rows = []
-        for b in blocks_of(c):
-            rows += split(s2, (b,), 0, 16)
-        turned = jnp.concatenate(rows, axis=0).T
+    loop(0, BLK, stage_l1x)
+    finish_l1()
+
+    def stage_y3(c):
+        rows = []
         for g in range(4):
-            t3[c, g, pl.ds(0, 32), :] = turned[32 * g : 32 * g + 32]
-
-    hx3.wait_recv()
-    loop(0, GRP, stage_x3)
-    hy3 = remote(
-        t3.at[:, :, pl.ds(0, HR)], t3.at[:, :, pl.ds(32, HR)], y_prev
-    )
-    hy3.start()
-
-    loop(0, BLK // 2, stage_l1x)
-
-    for copy in f2x:
+            t3[c, g, 6:8, :] = t3_r[c, g, :, :]
+            p3[c, g, 7:8, :] = f3p_r[0, c, g, :, :]
+            p3[c, g, 24:25, :] = f3p_r[1, c, g, :, :]
+            low, high = split(t3, (c, g), 6, 24)
+            high = jnp.abs(high)
+            detail = jnp.maximum(high, roll(jnp.maximum(jnp.abs(low), high), 104, 1))
+            c3[c, g, :, :] = jnp.maximum(detail, p3[c, g, pl.ds(7, 24), :])
+            boxed = jnp.maximum(c3[c, g, pl.ds(0, 16), :], c3[c, g, pl.ds(1, 16), :])
+            rows.append(jnp.maximum(boxed, c3[c, g, pl.ds(2, 16), :]))
+        x3[c, :, :] = jnp.concatenate(rows + rows, axis=0).T
+
+    for copy in hy3 + f3p:
         copy.wait_recv()
-
-    def stage_l2x(c):
-        rows = []
-        for b in blocks_of(c):
-            c2[b, 7:8, :] = f2x_r[0, b, :, :]
-            c2[b, 40:41, :] = f2x_r[1, b, :, :]
-            rows.append(box_rows(c2, (b,), 32))
-        turned = jnp.concatenate(rows, axis=0).T
-        for g in range(4):
-            y2[c, g, pl.ds(8, 32), :] = turned[32 * g : 32 * g + 32]
-            f2y_s[0, c, g, :, :] = turned[32 * g : 32 * g + 1]
-            f2y_s[1, c, g, :, :] = turned[32 * g + 31 : 32 * g + 32]
-
-    loop(0, GRP, stage_l2x)
-    f2y = frames(f2y_s, f2y_r, y_prev, y_next)
-    for copy in f2y:
-        copy.start()
-
-    def stage_y3(c):
-        for g in range(4):
-            low, high = split(t3, (c, g), 0, 16)
-            high = jnp.abs(high)
-            detail = jnp.maximum(high, roll(jnp.maximum(jnp.abs(low), high), 112, 1))
-            detail = jnp.maximum(detail, pool_rows(p2, (c,), 32 * g, 16))
-            c3[c, g, pl.ds(8, 16), :] = detail
-            f3y_s[0, c, g, :, :] = detail[0:1]
-            f3y_s[1, c, g, :, :] = detail[15:16]
-
-    hy3.wait_recv()
-    loop(0, GRP, stage_y3)
-    f3y = frames(f3y_s, f3y_r, y_prev, y_next)
-    for copy in f3y:
-        copy.start()
-
-    loop(BLK // 2, BLK, stage_l1x)
-    finish_l1()
-
-    for copy in f3y:
-        copy.wait_recv()
-
-    def stage_l3y(c):
-        rows = []
-        for g in range(4):
-            c3[c, g, 7:8, :] = f3y_r[0, c, g, :, :]
-            c3[c, g, 24:25, :] = f3y_r[1, c, g, :, :]
-            rows.append(box_rows(c3, (c, g), 16))
-        turned = jnp.concatenate(rows + rows, axis=0).T
-        for k in range(4):
-            x3[c, k, pl.ds(8, 16), :] = turned[32 * k : 32 * k + 16]
-            f3x_s[0, c, k, :, :] = turned[32 * k : 32 * k + 1]
-            f3x_s[1, c, k, :, :] = turned[32 * k + 15 : 32 * k + 16]
-
-    loop(0, GRP, stage_l3y)
-    f3x = frames(f3x_s, f3x_r, x_prev, x_next)
-    for copy in f3x:
-        copy.start()
+    loop(0, TWO, stage_y3)
 
     for copy in f2y:
         copy.wait_recv()
 
     offsets = (0, HALF, BLK, HALF + BLK)
-    for c in range(GRP):
+    for c in range(QUAD):
         rows = []
         for g in range(4):
             y2[c, g, 7:8, :] = f2y_r[0, c, g, :, :]
@@ -415,32 +416,30 @@
 
     loop(0, 32, stage_o2)
 
-    for copy in f3x:
-        copy.wait_recv()
-    for c in range(GRP):
-        for k in range(min(4, BLK - 4 * c)):
-            x3[c, k, 7:8, :] = f3x_r[0, c, k, :, :]
-            x3[c, k, 24:25, :] = f3x_r[1, c, k, :, :]
-            block = box_rows(x3, (c, k), 16)
+    for c in range(TWO):
+        for k in range(2):
+            block = x3[c, pl.ds(64 * k, 16), :]
+            for shift in (1, 2):
+                block = jnp.maximum(block, x3[c, pl.ds(64 * k + shift, 16), :])
             for g in range(4):
                 spun = roll(block, 128 - 16 * g, 1) if g else block
-                w3[pl.ds(4 * c + k + offsets[g], 16, stride=PITCH), :] = spun
+                w3[pl.ds(2 * c + k + offsets[g], 16, stride=PITCH), :] = spun
 
     def stage_o3(x):
         o3[x, :, :] = planes_last(w3, x, 16)
 
     loop(0, 16, stage_o3)
 
-    for row in hx1 + hy1 + [hy2, f1y, [hx2], f1x, [hx3], f2x, [hy3], f2y, f3y, f3x]:
+    for row in hx1 + hy1 + [f1y, hx2, fp, f1x, hy3, f3p, f2y]:
         for copy in row:
             copy.wait_send()
 
 
 def shards(vorticity):
     f32 = jnp.float32
-    copies = 4 * len(CHUNKS) + len(CHUNKS) + 4 + 12
+    copies = 5 * len(CHUNKS) + 14
     rows = lambda *shape: pltpu.VMEM(shape, f32)
-    frame = lambda *shape: [pltpu.VMEM((2,) + shape + (1, 128), f32)] * 2
+    pair = lambda *shape: [rows(*shape, 128)] * 2
     o1, o2, o3 = pl.pallas_call(
         kernel,
         out_shape=[
@@ -455,26 +454,29 @@
             rows(Z, 136, 128),
             rows(HALF, 72, 128),
             rows(HALF, 80, 128),
-            rows(BLK, 2, 72, 128),
-            rows(BLK, 40, 128),
+            rows(BLK, 2, 88, 128),
+            rows(BLK, 56, 128),
+            rows(BLK, 56, 128),
             rows(BLK, 48, 128),
-            rows(BLK, 32, 128),
             rows(5, 128, 128),
-            rows(GRP, 4, 40, 128),
-            rows(GRP, 128, 128),
-            rows(GRP, 4, 32, 128),
+            rows(TWO, 4, 64, 128),
+            rows(TWO, 128, 128),
+            rows(TWO, 4, 32, 128),
+            rows(TWO, 4, 24, 128),
             rows(BLK, 2, 80, 128),
             rows(BLK + 2, 2, 64, 128),
-            rows(GRP, 4, 48, 128),
+            rows(QUAD, 4, 48, 128),
             rows(32 * PITCH, 128),
-            rows(GRP, 4, 32, 128),
+            rows(TWO, 128, 128),
             rows(16 * PITCH, 128),
-            *frame(HALF),
-            *frame(BLK, 2),
-            *frame(BLK),
-            *frame(GRP, 4),
-            *frame(GRP, 4),
-            *frame(GRP, 4),
+            *pair(HALF, 8),
+            rows(HALF, 16, 128),
+            *pair(2, HALF, 1),
+            *pair(2, BLK, 2, 1),
+            *pair(2, BLK, 2),
+            *pair(2, QUAD, 4, 1),
+            *pair(2, TWO, 4, 1),
+            *pair(TWO, 4, 2),
             pltpu.SemaphoreType.DMA((2 * len(CHUNKS),)),
             pltpu.SemaphoreType.DMA((copies,)),
             pltpu.SemaphoreType.DMA((copies,)),

time: 49.2 us -> 42.7 us (0.87)
  the two profiles are of different devices: /device:TPU:1 before, /device:TPU:6 now
where the time goes in v3:
time: 42.7 us; the launch traced here: 42.5 us
  Pallas kernels  39.4 us (92%)
  local copies, waits for them, and re-layouts  2.46 us (6%)
  between operations  0.64 us (1%)
    pallas_call x1, Pallas kernels, shards(): pl.pallas_call(kernel, out_shape=[jax.ShapeDtypeStruct((OUT, 64, 64), f32...  39.4 us
    unnamed x3, local copies, waits for them, and re-layouts  2.46 us

profile of v3, /device:TPU:6, one launch (start us, length us, event | category | flops | bytes accessed | tf_op | source)
XLA Modules:
  0.0 42.5 jit_solution(18011669941004523624)
XLA Ops:
  0.6 39.4 %shard_map.38 = (f32[36,64,64]{2,1,0:T(8,128)S(1)}, f32[32,32,36]{2,1,0:T(8,128)S(1)}, f32[16,16,36]{2,1,0:T(8,128)S(1)}) custom-call(f32[38,128,128]{2,1,0:T(8,128)} %v.1), custom_call_target="tpu_custom_call" | custom-call | tf_op jit(solution)/shard_map/pallas_call | solution.py:443
  40.0 1.0 %copy.7 = f32[36,64,64]{2,1,0:T(8,128)} copy(f32[36,64,64]{2,1,0:T(8,128)S(1)} %get-tuple-element.12) | data formatting | bytes 1179648
  41.0 0.8 %copy.8 = f32[36,32,32]{0,2,1:T(8,128)} copy(f32[36,32,32]{0,2,1:T(8,128)S(1)} %bitcast.2) | data formatting | bytes 294912
  41.8 0.7 %copy.9 = f32[36,16,16]{0,2,1:T(8,128)} copy(f32[36,16,16]{0,2,1:T(8,128)S(1)} %bitcast.3) | data formatting | bytes 73728

commit v4 on v3

--- a/solution.py
+++ b/solution.py
@@ -21,6 +21,7 @@
 BLK = 10
 QUAD = 3
 TWO = 5
+STRIPS = 3
 HR = 4
 OUT = Z - 2
 PITCH = 48
@@ -75,7 +76,8 @@
 def kernel(
     v, o1, o2, o3,
     vb, tb, s1, d1, t2, s2, c2, pc, p1, t3, p2, p3, c3, e1, eb, y2, w2, x3, w3,
-    lk_s, lk_r, lh, f1y_s, f1y_r, f1x_s, f1x_r, fp_s, fp_r, f2y_s, f2y_r, f3p_s, f3p_r, t3_s, t3_r,
+    lk_s, lk_r, lh, f1y_s, f1y_r, f1x_s, f1x_r, fp_s, fp_r, sl, us, ts, ss, ds, ta, tx,
+    f2y_s, f2y_r, f3p_s, f3p_r, t3_s, t3_r,
     in_sem, send_sem, recv_sem,
 ):
     nx, ny = lax.axis_size("gx"), lax.axis_size("gy")
@@ -117,6 +119,10 @@
     for row in loads:
         for copy in row:
             copy.start()
+    edge = pltpu.make_async_copy(
+        v.at[:, pl.ds(0, 8)], sl.at[:, pl.ds(8, 8)], in_sem.at[2 * len(CHUNKS)]
+    )
+    edge.start()
 
     barrier = pltpu.get_barrier_semaphore()
     for device in (x_prev, x_next, y_prev, y_next):
@@ -134,6 +140,8 @@
         for copy in row:
             copy.start()
         hx1.append(row)
+    hs1 = remote(v.at[:, pl.ds(120, 8)], sl.at[:, pl.ds(0, 8)], x_next)
+    hs1.start()
 
     def stage_x1(p):
         lows, highs = [], []
@@ -172,6 +180,59 @@
         copy.start()
         hy1.append(row + [copy])
 
+    def stage_xs(p):
+        low, high = split(sl, (jnp.minimum(p, Z - 1),), 0, 4)
+        us[p, 0:4, :] = low
+        us[p, 4:8, :] = high
+
+    def stage_ts(i):
+        ts[i, pl.ds(8, 128), :] = us[pl.ds(16 * i, 16)].reshape(128, 128).T
+
+    edge.wait()
+    hs1.wait_recv()
+    loop(0, 16 * STRIPS, stage_xs)
+    loop(0, STRIPS, stage_ts)
+    hs2 = [
+        remote(ts.at[:, pl.ds(8, 16)], ts.at[:, pl.ds(136, 16)], y_prev),
+        remote(ts.at[:, pl.ds(128, 8)], ts.at[:, pl.ds(0, 8)], y_next),
+    ]
+    for copy in hs2:
+        copy.start()
+
+    def stage_ys(i):
+        low, high = split(ts, (i,), 6, 70)
+        high = jnp.abs(high)
+        ss[i, pl.ds(7, 70), :] = low
+        ds[i, pl.ds(7, 70), :] = jnp.maximum(
+            high, roll(jnp.maximum(jnp.abs(low), high), 124, 1)
+        )
+
+    def stage_zs(i):
+        low, high = split(ss, (i,), 8, 32)
+        pooled = pool_rows(ds, (i,), 8, 32)
+        turned = jnp.concatenate([low, high, pooled, pooled], axis=0).T
+        ta[pl.ds(16 * i, 16)] = turned.reshape(16, 8, 128)
+        boxed = box_rows(ds, (i,), 64)
+        turned = jnp.concatenate([boxed, boxed], axis=0).T
+        tx[pl.ds(16 * i, 16)] = turned.reshape(16, 8, 128)
+
+    def stage_left(b):
+        four, two = lane_ids(4), lane_ids(2)
+        pooled = []
+        for k in range(2):
+            p = b + HALF * k
+            t2[b, k, 4:8, :] = jnp.where(
+                four < 64, ta[p, 0:4, :], roll(ta[p + BLK, 0:4, :], 64, 1)
+            )
+            e1[b, k, 7:8, :] = jnp.where(
+                lane_ids(1) < 64, tx[p, 3:4, :], tx[p + BLK, 3:4, :]
+            )
+        for p in (b, b + HALF, b + BLK, b + HALF + BLK):
+            pooled.append(pool_rows(ta, (p,), 0, 2))
+        lower = roll(jnp.where(two < 96, pooled[0], pooled[1]), 64, 1)
+        upper = jnp.where(two < 96, pooled[2], pooled[3])
+        pc[b, 6:8, :] = jnp.where(two < 64, lower, upper)
+
     first = lane_ids(32) < 64
 
     def stage_y1(q):
@@ -222,8 +283,7 @@
             (b + 5, jnp.where(quarter, roll(pool_a, 96, 1), pool_b)),
         ):
             pc[block, pl.ds(8, 32), :] = pooled
-            fp_s[0, block, :, :] = pooled[0:2]
-            fp_s[1, block, :, :] = pooled[30:32]
+            fp_s[block, :, :] = pooled[0:2]
 
     def stage_y2(b):
         rows = []
@@ -234,14 +294,11 @@
         t2[b, 1, pl.ds(8, 64), :] = turned[64:]
 
     loop(0, BLK, stage_y2)
-    hx2 = [
-        remote(t2.at[:, :, pl.ds(8, 16)], t2.at[:, :, pl.ds(72, 16)], x_prev),
-        remote(t2.at[:, :, pl.ds(64, 8)], t2.at[:, :, pl.ds(0, 8)], x_next),
-    ]
+    hx2 = [remote(t2.at[:, :, pl.ds(8, 16)], t2.at[:, :, pl.ds(72, 16)], x_prev)]
     for copy in hx2:
         copy.start()
     loop(0, 5, stage_p1)
-    fp = frames(fp_s, fp_r, x_prev, x_next)
+    fp = [remote(fp_s, fp_r, x_prev)]
     for copy in fp:
         copy.start()
 
@@ -257,19 +314,23 @@
         turned = jnp.concatenate(rows, axis=0).T
         for k in range(2):
             e1[b, k, pl.ds(8, 64), :] = turned[64 * k : 64 * k + 64]
-            f1x_s[0, b, k, :, :] = turned[64 * k : 64 * k + 1]
-            f1x_s[1, b, k, :, :] = turned[64 * k + 63 : 64 * k + 64]
+            f1x_s[b, k, :, :] = turned[64 * k : 64 * k + 1]
 
     loop(0, BLK, stage_l1y)
-    f1x = frames(f1x_s, f1x_r, x_prev, x_next)
+    f1x = [remote(f1x_s, f1x_r, x_prev)]
     for copy in f1x:
         copy.start()
 
+    for copy in hs2:
+        copy.wait_recv()
+    loop(0, STRIPS, stage_ys)
+    loop(0, STRIPS, stage_zs)
+    loop(0, BLK, stage_left)
+
     wide = lax.rem(lane_ids(40), 64) < 32
 
     def stage_x2(b):
-        pc[b, 6:8, :] = fp_r[0, b, :, :]
-        pc[b, 40:42, :] = fp_r[1, b, :, :]
+        pc[b, 40:42, :] = fp_r[b, :, :]
         lows, details = [], []
         for k in range(2):
             low, high = split(t2, (b, k), 4, 40)
@@ -340,8 +401,7 @@
 
     def stage_l1x(b):
         for k in range(2):
-            e1[b, k, 7:8, :] = f1x_r[0, b, k, :, :]
-            e1[b, k, 72:73, :] = f1x_r[1, b, k, :, :]
+            e1[b, k, 72:73, :] = f1x_r[b, k, :, :]
             eb[b, k, :, :] = box_rows(e1, (b, k), 64)
 
     def deep(b, k):
@@ -430,9 +490,20 @@
 
     loop(0, 16, stage_o3)
 
-    for row in hx1 + hy1 + [f1y, hx2, fp, f1x, hy3, f3p, f2y]:
+    for row in hx1 + hy1 + [[hs1], hs2, f1y, hx2, fp, f1x, hy3, f3p, f2y]:
         for copy in row:
             copy.wait_send()
+
+
+def write_out(a1, a2, a3, b1, b2, b3, sems):
+    copies = [
+        pltpu.make_async_copy(src, dst, sems.at[k])
+        for k, (src, dst) in enumerate(((a1, b1), (a2, b2), (a3, b3)))
+    ]
+    for copy in copies:
+        copy.start()
+    for copy in copies:
+        copy.wait()
 
 
 def shards(vorticity):
@@ -440,13 +511,14 @@
     copies = 5 * len(CHUNKS) + 14
     rows = lambda *shape: pltpu.VMEM(shape, f32)
     pair = lambda *shape: [rows(*shape, 128)] * 2
-    o1, o2, o3 = pl.pallas_call(
+    results = [
+        jax.ShapeDtypeStruct((OUT, 64, 64), f32),
+        jax.ShapeDtypeStruct((32, 32, OUT), f32),
+        jax.ShapeDtypeStruct((16, 16, OUT), f32),
+    ]
+    inner = pl.pallas_call(
         kernel,
-        out_shape=[
-            jax.ShapeDtypeStruct((OUT, 64, 64), f32),
-            jax.ShapeDtypeStruct((32, 32, OUT), f32),
-            jax.ShapeDtypeStruct((16, 16, OUT), f32),
-        ],
+        out_shape=results,
         in_specs=[pl.BlockSpec(memory_space=pltpu.HBM)],
         out_specs=[pl.BlockSpec(memory_space=pltpu.VMEM)] * 3,
         scratch_shapes=[
@@ -472,12 +544,19 @@
             *pair(HALF, 8),
             rows(HALF, 16, 128),
             *pair(2, HALF, 1),
-            *pair(2, BLK, 2, 1),
-            *pair(2, BLK, 2),
+            *pair(BLK, 2, 1),
+            *pair(BLK, 2),
+            rows(Z, 16, 128),
+            rows(16 * STRIPS, 8, 128),
+            rows(STRIPS, 152, 128),
+            rows(STRIPS, 80, 128),
+            rows(STRIPS, 80, 128),
+            rows(16 * STRIPS, 8, 128),
+            rows(16 * STRIPS, 8, 128),
             *pair(2, QUAD, 4, 1),
             *pair(2, TWO, 4, 1),
             *pair(TWO, 4, 2),
-            pltpu.SemaphoreType.DMA((2 * len(CHUNKS),)),
+            pltpu.SemaphoreType.DMA((2 * len(CHUNKS) + 1,)),
             pltpu.SemaphoreType.DMA((copies,)),
             pltpu.SemaphoreType.DMA((copies,)),
         ],
@@ -485,6 +564,14 @@
             collective_id=0, has_side_effects=True, vmem_limit_bytes=51 * 2**20
         ),
     )(vorticity)
+    o1, o2, o3 = pl.pallas_call(
+        write_out,
+        out_shape=results,
+        in_specs=[pl.BlockSpec(memory_space=pl.ANY)] * 3,
+        out_specs=[pl.BlockSpec(memory_space=pl.ANY)] * 3,
+        scratch_shapes=[pltpu.SemaphoreType.DMA((3,))],
+        compiler_params=pltpu.CompilerParams(vmem_limit_bytes=2**20),
+    )(*inner)
     return o1, jnp.transpose(o2, (2, 0, 1)), jnp.transpose(o3, (2, 0, 1))
 
 

time: 42.7 us -> 39.5 us (0.925)
  local copies, waits for them, and re-layouts: 2.46 us -> 0 us
  Pallas kernels: 39.4 us -> 38.7 us
    unnamed x3 -> x0, local copies, waits for them, and re-layouts: 2.46 us -> none
    pallas_call x1 -> x2, Pallas kernels: 39.4 us -> 38.7 us  [the longest x1 37.5 us: shards(): pl.pallas_call(kernel, out_shape=results, in_specs=[pl.BlockSpec(memory_s...]
where the time goes in v4:
time: 39.5 us; the launch traced here: 39.3 us
  Pallas kernels  38.7 us (98%)
  between operations  0.64 us (2%)
    pallas_call x1, Pallas kernels, shards(): pl.pallas_call(kernel, out_shape=results, in_specs=[pl.BlockSpec(memory_s...  37.5 us
    pallas_call x1, Pallas kernels, shards(): pl.pallas_call(write_out, out_shape=results, in_specs=[pl.BlockSpec(memor...  1.24 us

profile of v4, /device:TPU:6, one launch (start us, length us, event | category | flops | bytes accessed | tf_op | source)
XLA Modules:
  0.0 39.3 jit_solution(13461796322986029517)
XLA Ops:
  0.6 37.5 %shard_map.38 = (f32[36,64,64]{2,1,0:T(8,128)S(1)}, f32[32,32,36]{2,1,0:T(8,128)S(1)}, f32[16,16,36]{2,1,0:T(8,128)S(1)}) custom-call(f32[38,128,128]{2,1,0:T(8,128)} %v.1), custom_call_target="tpu_custom_call" | custom-call | tf_op jit(solution)/shard_map/pallas_call | solution.py:519
  38.1 1.2 %shard_map.39 = (f32[36,64,64]{2,1,0:T(8,128)}, f32[32,32,36]{2,1,0:T(8,128)}, f32[16,16,36]{2,1,0:T(8,128)}) custom-call(f32[36,64,64]{2,1,0:T(8,128)S(1)} %get-tuple-element.9.a1, f32[32,32,36]{2,1,0:T(8,128)S(1)} %get-tuple-element.10.a2, f32[16,16,36]{2,1,0:T(8,128)S(1)} %get-tuple-element.11.a3), custom_call_target="tpu_custom_call" | custom-call | tf_op jit(solution)/shard_map/pallas_call | solution.py:567

commit v5 on v4

--- a/solution.py
+++ b/solution.py
@@ -127,21 +127,28 @@
     barrier = pltpu.get_barrier_semaphore()
     for device in (x_prev, x_next, y_prev, y_next):
         pl.semaphore_signal(barrier, inc=1, device_id=device, device_id_type=MESH)
-    pl.semaphore_wait(barrier, 4)
 
     for pieces in spans:
-        row = [
+        hx1.append([
             remote(
                 v.at[pl.ds(a, b - a), pl.ds(0, HR)],
                 vb.at[pl.ds(a, b - a), pl.ds(128, HR)], x_prev,
             )
             for a, b in pieces
+        ])
+    hs1 = remote(v.at[:, pl.ds(120, 8)], sl.at[:, pl.ds(0, 8)], x_next)
+    for (q0, q1), pieces in zip(CHUNKS, spans):
+        row = [
+            remote(
+                tb.at[pl.ds(a, b - a), pl.ds(0, HR)],
+                tb.at[pl.ds(a, b - a), pl.ds(128, HR)], y_prev,
+            )
+            for a, b in pieces
         ]
-        for copy in row:
-            copy.start()
-        hx1.append(row)
-    hs1 = remote(v.at[:, pl.ds(120, 8)], sl.at[:, pl.ds(0, 8)], x_next)
-    hs1.start()
+        row.append(
+            remote(lk_s.at[pl.ds(q0, q1 - q0)], lk_r.at[pl.ds(q0, q1 - q0)], y_prev)
+        )
+        hy1.append(row)
 
     def stage_x1(p):
         lows, highs = [], []
@@ -158,27 +165,43 @@
     def stage_k1(q):
         lk_s[q, :, :] = both(tb, q, HR, 8)
 
-    for number, pieces in enumerate(spans):
+    def begin(number):
         for copy in loads[number]:
             copy.wait()
         for copy in hx1[number]:
             copy.wait_recv()
-        for a, b in pieces:
+        for a, b in spans[number]:
             loop(a, b, stage_x1)
-        row = [
-            remote(
-                tb.at[pl.ds(a, b - a), pl.ds(0, HR)],
-                tb.at[pl.ds(a, b - a), pl.ds(128, HR)], y_prev,
-            )
-            for a, b in pieces
-        ]
+        loop(*CHUNKS[number], stage_k1)
+
+    def send(number):
+        for copy in hy1[number]:
+            copy.start()
+
+    even = lax.rem(ix, 2) == 0
+
+    @pl.when(even)
+    def _():
+        for number in range(len(CHUNKS)):
+            begin(number)
+
+    pl.semaphore_wait(barrier, 4)
+
+    hs1.start()
+    for row in hx1:
         for copy in row:
             copy.start()
-        q0, q1 = CHUNKS[number]
-        loop(q0, q1, stage_k1)
-        copy = remote(lk_s.at[pl.ds(q0, q1 - q0)], lk_r.at[pl.ds(q0, q1 - q0)], y_prev)
-        copy.start()
-        hy1.append(row + [copy])
+
+    @pl.when(even)
+    def _():
+        for number in range(len(CHUNKS)):
+            send(number)
+
+    @pl.when(jnp.logical_not(even))
+    def _():
+        for number in range(len(CHUNKS)):
+            begin(number)
+            send(number)
 
     def stage_xs(p):
         low, high = split(sl, (jnp.minimum(p, Z - 1),), 0, 4)
@@ -302,25 +325,6 @@
     for copy in fp:
         copy.start()
 
-    for copy in f1y:
-        copy.wait_recv()
-
-    def stage_l1y(b):
-        rows = []
-        for q in (b, b + BLK):
-            d1[q, 7:8, :] = f1y_r[0, q, :, :]
-            d1[q, 72:73, :] = f1y_r[1, q, :, :]
-            rows.append(box_rows(d1, (q,), 64))
-        turned = jnp.concatenate(rows, axis=0).T
-        for k in range(2):
-            e1[b, k, pl.ds(8, 64), :] = turned[64 * k : 64 * k + 64]
-            f1x_s[b, k, :, :] = turned[64 * k : 64 * k + 1]
-
-    loop(0, BLK, stage_l1y)
-    f1x = [remote(f1x_s, f1x_r, x_prev)]
-    for copy in f1x:
-        copy.start()
-
     for copy in hs2:
         copy.wait_recv()
     loop(0, STRIPS, stage_ys)
@@ -394,6 +398,25 @@
     loop(0, QUAD, stage_l2x)
     f2y = frames(f2y_s, f2y_r, y_prev, y_next)
     for copy in f2y:
+        copy.start()
+
+    for copy in f1y:
+        copy.wait_recv()
+
+    def stage_l1y(b):
+        rows = []
+        for q in (b, b + BLK):
+            d1[q, 7:8, :] = f1y_r[0, q, :, :]
+            d1[q, 72:73, :] = f1y_r[1, q, :, :]
+            rows.append(box_rows(d1, (q,), 64))
+        turned = jnp.concatenate(rows, axis=0).T
+        for k in range(2):
+            e1[b, k, pl.ds(8, 64), :] = turned[64 * k : 64 * k + 64]
+            f1x_s[b, k, :, :] = turned[64 * k : 64 * k + 1]
+
+    loop(0, BLK, stage_l1y)
+    f1x = [remote(f1x_s, f1x_r, x_prev)]
+    for copy in f1x:
         copy.start()
 
     for copy in f1x:
@@ -451,6 +474,17 @@
         copy.wait_recv()
 
     offsets = (0, HALF, BLK, HALF + BLK)
+
+    def spread(block, w, unit, b):
+        n = block.shape[0]
+        spun = [roll(block, unit * d, 1) if d else block for d in range(4)]
+        group = lax.rem(lane_ids(n) // unit, 4)
+        for g in range(4):
+            full = spun[(3 - g) % 4]
+            for r in range(3):
+                full = jnp.where(group == r, spun[(r - g) % 4], full)
+            w[pl.ds(b + offsets[g], n, stride=PITCH), :] = full
+
     for c in range(QUAD):
         rows = []
         for g in range(4):
@@ -460,35 +494,32 @@
         turned = jnp.concatenate(rows, axis=0).T
         for k in range(min(4, BLK - 4 * c)):
             block = turned[32 * k : 32 * k + 32]
-            for g in range(4):
-                spun = roll(block, 128 - 32 * g, 1) if g else block
-                w2[pl.ds(4 * c + k + offsets[g], 32, stride=PITCH), :] = spun
-
-    def planes_last(w, x, n):
-        start = pl.multiple_of(x * PITCH, 8)
-        deepest = w[pl.ds(start, 40), :]
-        for shift in (1, 2):
-            deepest = jnp.maximum(deepest, w[pl.ds(start + shift, 40), :])
-        return deepest.T[:n, :OUT]
-
-    def stage_o2(x):
-        o2[x, :, :] = planes_last(w2, x, 32)
-
-    loop(0, 32, stage_o2)
+            spread(block, w2, 32, 4 * c + k)
+
+    def planes_last(w, out, m, unit):
+        count = 128 // unit
+        group = lane_ids(40) // unit
+        merged = None
+        for r in range(count):
+            start = pl.multiple_of((m * count + r) * PITCH, 8)
+            deepest = w[pl.ds(start, 40), :]
+            for shift in (1, 2):
+                deepest = jnp.maximum(deepest, w[pl.ds(start + shift, 40), :])
+            merged = deepest if r == 0 else jnp.where(group == r, deepest, merged)
+        turned = merged.T
+        for r in range(count):
+            out[m * count + r, :, :] = turned[unit * r : unit * r + unit, :OUT]
+
+    loop(0, 8, lambda m: planes_last(w2, o2, m, 32))
 
     for c in range(TWO):
         for k in range(2):
             block = x3[c, pl.ds(64 * k, 16), :]
             for shift in (1, 2):
                 block = jnp.maximum(block, x3[c, pl.ds(64 * k + shift, 16), :])
-            for g in range(4):
-                spun = roll(block, 128 - 16 * g, 1) if g else block
-                w3[pl.ds(2 * c + k + offsets[g], 16, stride=PITCH), :] = spun
-
-    def stage_o3(x):
-        o3[x, :, :] = planes_last(w3, x, 16)
-
-    loop(0, 16, stage_o3)
+            spread(block, w3, 16, 2 * c + k)
+
+    loop(0, 2, lambda m: planes_last(w3, o3, m, 16))
 
     for row in hx1 + hy1 + [[hs1], hs2, f1y, hx2, fp, f1x, hy3, f3p, f2y]:
         for copy in row:

time: 39.5 us -> 37 us (0.937)
  Pallas kernels: 38.7 us -> 36.2 us
    pallas_call x1, Pallas kernels: 37.5 us -> 35 us  [shards(): pl.pallas_call(kernel, out_shape=results, in_specs=[pl.BlockSpec(memory_s...]
where the time goes in v5:
time: 37 us; the launch traced here: 36.9 us
  Pallas kernels  36.2 us (98%)
  between operations  0.64 us (2%)
    pallas_call x1, Pallas kernels, shards(): pl.pallas_call(kernel, out_shape=results, in_specs=[pl.BlockSpec(memory_s...  35 us
    pallas_call x1, Pallas kernels, shards(): pl.pallas_call(write_out, out_shape=results, in_specs=[pl.BlockSpec(memor...  1.24 us

profile of v5, /device:TPU:6, one launch (start us, length us, event | category | flops | bytes accessed | tf_op | source)
XLA Modules:
  0.0 36.9 jit_solution(14327053216710104121)
XLA Ops:
  0.6 35.0 %shard_map.38 = (f32[36,64,64]{2,1,0:T(8,128)S(1)}, f32[32,32,36]{2,1,0:T(8,128)S(1)}, f32[16,16,36]{2,1,0:T(8,128)S(1)}) custom-call(f32[38,128,128]{2,1,0:T(8,128)} %v.1), custom_call_target="tpu_custom_call" | custom-call | tf_op jit(solution)/shard_map/pallas_call | solution.py:550
  35.6 1.2 %shard_map.39 = (f32[36,64,64]{2,1,0:T(8,128)}, f32[32,32,36]{2,1,0:T(8,128)}, f32[16,16,36]{2,1,0:T(8,128)}) custom-call(f32[36,64,64]{2,1,0:T(8,128)S(1)} %get-tuple-element.9.a1, f32[32,32,36]{2,1,0:T(8,128)S(1)} %get-tuple-element.10.a2, f32[16,16,36]{2,1,0:T(8,128)S(1)} %get-tuple-element.11.a3), custom_call_target="tpu_custom_call" | custom-call | tf_op jit(solution)/shard_map/pallas_call | solution.py:598

commit v6 on v5

--- a/solution.py
+++ b/solution.py
@@ -105,7 +105,7 @@
     spans = []
     for q0, q1 in CHUNKS:
         spans.append(((q0, q1), (q0 + HALF, min(q1 + HALF, Z))))
-    loads, hx1, hy1 = [], [], []
+    loads, hx1, hy1, hk1 = [], [], [], []
     for number, pieces in enumerate(spans):
         row = []
         for part, (a, b) in enumerate(pieces):
@@ -145,10 +145,10 @@
             )
             for a, b in pieces
         ]
-        row.append(
+        hy1.append(row)
+        hk1.append(
             remote(lk_s.at[pl.ds(q0, q1 - q0)], lk_r.at[pl.ds(q0, q1 - q0)], y_prev)
         )
-        hy1.append(row)
 
     def stage_x1(p):
         lows, highs = [], []
@@ -172,7 +172,6 @@
             copy.wait_recv()
         for a, b in spans[number]:
             loop(a, b, stage_x1)
-        loop(*CHUNKS[number], stage_k1)
 
     def send(number):
         for copy in hy1[number]:
@@ -184,6 +183,7 @@
     def _():
         for number in range(len(CHUNKS)):
             begin(number)
+            loop(*CHUNKS[number], stage_k1)
 
     pl.semaphore_wait(barrier, 4)
 
@@ -196,12 +196,16 @@
     def _():
         for number in range(len(CHUNKS)):
             send(number)
+        for copy in hk1:
+            copy.start()
 
     @pl.when(jnp.logical_not(even))
     def _():
         for number in range(len(CHUNKS)):
             begin(number)
             send(number)
+            loop(*CHUNKS[number], stage_k1)
+            hk1[number].start()
 
     def stage_xs(p):
         low, high = split(sl, (jnp.minimum(p, Z - 1),), 0, 4)
@@ -289,10 +293,12 @@
         for copy in hy1[number]:
             copy.wait_recv()
         loop(q0, q1, stage_y1)
-        loop(q0, q1, stage_k2)
     f1y = frames(f1y_s, f1y_r, y_prev, y_next)
     for copy in f1y:
         copy.start()
+    for copy in hk1:
+        copy.wait_recv()
+    loop(0, HALF, stage_k2)
 
     quarter = lax.rem(lane_ids(32), 64) < 32
 
@@ -351,6 +357,19 @@
         copy.wait_recv()
     loop(0, BLK, stage_x2)
 
+    def stage_l2x(c):
+        rows = [box_rows(c2, (jnp.minimum(4 * c + k, BLK - 1),), 32) for k in range(4)]
+        turned = jnp.concatenate(rows, axis=0).T
+        for g in range(4):
+            y2[c, g, pl.ds(8, 32), :] = turned[32 * g : 32 * g + 32]
+            f2y_s[0, c, g, :, :] = turned[32 * g : 32 * g + 1]
+            f2y_s[1, c, g, :, :] = turned[32 * g + 31 : 32 * g + 32]
+
+    loop(0, QUAD, stage_l2x)
+    f2y = frames(f2y_s, f2y_r, y_prev, y_next)
+    for copy in f2y:
+        copy.start()
+
     def stage_x3(c):
         rows = []
         for k in range(2):
@@ -387,19 +406,6 @@
     for copy in f3p:
         copy.start()
 
-    def stage_l2x(c):
-        rows = [box_rows(c2, (jnp.minimum(4 * c + k, BLK - 1),), 32) for k in range(4)]
-        turned = jnp.concatenate(rows, axis=0).T
-        for g in range(4):
-            y2[c, g, pl.ds(8, 32), :] = turned[32 * g : 32 * g + 32]
-            f2y_s[0, c, g, :, :] = turned[32 * g : 32 * g + 1]
-            f2y_s[1, c, g, :, :] = turned[32 * g + 31 : 32 * g + 32]
-
-    loop(0, QUAD, stage_l2x)
-    f2y = frames(f2y_s, f2y_r, y_prev, y_next)
-    for copy in f2y:
-        copy.start()
-
     for copy in f1y:
         copy.wait_recv()
 
@@ -418,6 +424,48 @@
     f1x = [remote(f1x_s, f1x_r, x_prev)]
     for copy in f1x:
         copy.start()
+
+    for copy in f2y:
+        copy.wait_recv()
+
+    offsets = (0, HALF, BLK, HALF + BLK)
+
+    def spread(block, w, unit, b):
+        n = block.shape[0]
+        spun = [roll(block, unit * d, 1) if d else block for d in range(4)]
+        group = lax.rem(lane_ids(n) // unit, 4)
+        for g in range(4):
+            full = spun[(3 - g) % 4]
+            for r in range(3):
+                full = jnp.where(group == r, spun[(r - g) % 4], full)
+            w[pl.ds(b + offsets[g], n, stride=PITCH), :] = full
+
+    for c in range(QUAD):
+        rows = []
+        for g in range(4):
+            y2[c, g, 7:8, :] = f2y_r[0, c, g, :, :]
+            y2[c, g, 40:41, :] = f2y_r[1, c, g, :, :]
+            rows.append(box_rows(y2, (c, g), 32))
+        turned = jnp.concatenate(rows, axis=0).T
+        for k in range(min(4, BLK - 4 * c)):
+            block = turned[32 * k : 32 * k + 32]
+            spread(block, w2, 32, 4 * c + k)
+
+    def planes_last(w, out, m, unit):
+        count = 128 // unit
+        group = lane_ids(40) // unit
+        merged = None
+        for r in range(count):
+            start = pl.multiple_of((m * count + r) * PITCH, 8)
+            deepest = w[pl.ds(start, 40), :]
+            for shift in (1, 2):
+                deepest = jnp.maximum(deepest, w[pl.ds(start + shift, 40), :])
+            merged = deepest if r == 0 else jnp.where(group == r, deepest, merged)
+        turned = merged.T
+        for r in range(count):
+            out[m * count + r, :, :] = turned[unit * r : unit * r + unit, :OUT]
+
+    loop(0, 8, lambda m: planes_last(w2, o2, m, 32))
 
     for copy in f1x:
         copy.wait_recv()
@@ -470,48 +518,6 @@
         copy.wait_recv()
     loop(0, TWO, stage_y3)
 
-    for copy in f2y:
-        copy.wait_recv()
-
-    offsets = (0, HALF, BLK, HALF + BLK)
-
-    def spread(block, w, unit, b):
-        n = block.shape[0]
-        spun = [roll(block, unit * d, 1) if d else block for d in range(4)]
-        group = lax.rem(lane_ids(n) // unit, 4)
-        for g in range(4):
-            full = spun[(3 - g) % 4]
-            for r in range(3):
-                full = jnp.where(group == r, spun[(r - g) % 4], full)
-            w[pl.ds(b + offsets[g], n, stride=PITCH), :] = full
-
-    for c in range(QUAD):
-        rows = []
-        for g in range(4):
-            y2[c, g, 7:8, :] = f2y_r[0, c, g, :, :]
-            y2[c, g, 40:41, :] = f2y_r[1, c, g, :, :]
-            rows.append(box_rows(y2, (c, g), 32))
-        turned = jnp.concatenate(rows, axis=0).T
-        for k in range(min(4, BLK - 4 * c)):
-            block = turned[32 * k : 32 * k + 32]
-            spread(block, w2, 32, 4 * c + k)
-
-    def planes_last(w, out, m, unit):
-        count = 128 // unit
-        group = lane_ids(40) // unit
-        merged = None
-        for r in range(count):
-            start = pl.multiple_of((m * count + r) * PITCH, 8)
-            deepest = w[pl.ds(start, 40), :]
-            for shift in (1, 2):
-                deepest = jnp.maximum(deepest, w[pl.ds(start + shift, 40), :])
-            merged = deepest if r == 0 else jnp.where(group == r, deepest, merged)
-        turned = merged.T
-        for r in range(count):
-            out[m * count + r, :, :] = turned[unit * r : unit * r + unit, :OUT]
-
-    loop(0, 8, lambda m: planes_last(w2, o2, m, 32))
-
     for c in range(TWO):
         for k in range(2):
             block = x3[c, pl.ds(64 * k, 16), :]
@@ -521,7 +527,7 @@
 
     loop(0, 2, lambda m: planes_last(w3, o3, m, 16))
 
-    for row in hx1 + hy1 + [[hs1], hs2, f1y, hx2, fp, f1x, hy3, f3p, f2y]:
+    for row in hx1 + hy1 + [hk1, [hs1], hs2, f1y, hx2, fp, f1x, hy3, f3p, f2y]:
         for copy in row:
             copy.wait_send()
 

time: 37 us -> 37.3 us (level)
  no operation moved by 1% of the time
where the time goes in v6:
time: 37.3 us; the launch traced here: 37.1 us
  Pallas kernels  36.5 us (98%)
  between operations  0.64 us (2%)
    pallas_call x1, Pallas kernels, shards(): pl.pallas_call(kernel, out_shape=results, in_specs=[pl.BlockSpec(memory_s...  35.2 us
    pallas_call x1, Pallas kernels, shards(): pl.pallas_call(write_out, out_shape=results, in_specs=[pl.BlockSpec(memor...  1.24 us

profile of v6, /device:TPU:6, one launch (start us, length us, event | category | flops | bytes accessed | tf_op | source)
XLA Modules:
  0.0 37.1 jit_solution(5377773810323595656)
XLA Ops:
  0.6 35.2 %shard_map.38 = (f32[36,64,64]{2,1,0:T(8,128)S(1)}, f32[32,32,36]{2,1,0:T(8,128)S(1)}, f32[16,16,36]{2,1,0:T(8,128)S(1)}) custom-call(f32[38,128,128]{2,1,0:T(8,128)} %v.1), custom_call_target="tpu_custom_call" | custom-call | tf_op jit(solution)/shard_map/pallas_call | solution.py:556
  35.8 1.2 %shard_map.39 = (f32[36,64,64]{2,1,0:T(8,128)}, f32[32,32,36]{2,1,0:T(8,128)}, f32[16,16,36]{2,1,0:T(8,128)}) custom-call(f32[36,64,64]{2,1,0:T(8,128)S(1)} %get-tuple-element.9.a1, f32[32,32,36]{2,1,0:T(8,128)S(1)} %get-tuple-element.10.a2, f32[16,16,36]{2,1,0:T(8,128)S(1)} %get-tuple-element.11.a3), custom_call_target="tpu_custom_call" | custom-call | tf_op jit(solution)/shard_map/pallas_call | solution.py:604

commit v7 on v6

--- a/solution.py
+++ b/solution.py
@@ -25,7 +25,7 @@
 HR = 4
 OUT = Z - 2
 PITCH = 48
-UNROLL = 5
+UNROLL = 10
 CHUNKS = ((0, 10), (10, 20))
 MESH = pl.DeviceIdType.MESH
 roll = pltpu.roll

time: 37.3 us -> 36.7 us (0.984)
  Pallas kernels: 36.5 us -> 35.9 us
    pallas_call x1, Pallas kernels: 35.2 us -> 34.6 us  [shards(): pl.pallas_call(kernel, out_shape=results, in_specs=[pl.BlockSpec(memory_s...]
where the time goes in v7:
time: 36.7 us; the launch traced here: 36.5 us
  Pallas kernels  35.9 us (98%)
  between operations  0.64 us (2%)
    pallas_call x1, Pallas kernels, shards(): pl.pallas_call(kernel, out_shape=results, in_specs=[pl.BlockSpec(memory_s...  34.6 us
    pallas_call x1, Pallas kernels, shards(): pl.pallas_call(write_out, out_shape=results, in_specs=[pl.BlockSpec(memor...  1.24 us

profile of v7, /device:TPU:6, one launch (start us, length us, event | category | flops | bytes accessed | tf_op | source)
XLA Modules:
  0.0 36.5 jit_solution(2144937957474008610)
XLA Ops:
  0.6 34.6 %shard_map.38 = (f32[36,64,64]{2,1,0:T(8,128)S(1)}, f32[32,32,36]{2,1,0:T(8,128)S(1)}, f32[16,16,36]{2,1,0:T(8,128)S(1)}) custom-call(f32[38,128,128]{2,1,0:T(8,128)} %v.1), custom_call_target="tpu_custom_call" | custom-call | tf_op jit(solution)/shard_map/pallas_call | solution.py:556
  35.3 1.2 %shard_map.39 = (f32[36,64,64]{2,1,0:T(8,128)}, f32[32,32,36]{2,1,0:T(8,128)}, f32[16,16,36]{2,1,0:T(8,128)}) custom-call(f32[36,64,64]{2,1,0:T(8,128)S(1)} %get-tuple-element.9.a1, f32[32,32,36]{2,1,0:T(8,128)S(1)} %get-tuple-element.10.a2, f32[16,16,36]{2,1,0:T(8,128)S(1)} %get-tuple-element.11.a3), custom_call_target="tpu_custom_call" | custom-call | tf_op jit(solution)/shard_map/pallas_call | solution.py:604
